TPU v7x, 32 devices: a whole 2x2x4 slice. The times are simulated.
32 devices in a mesh: orb: 32 (over z, y, x, core).
Axes of the slice: x: 2, y: 2, z: 4, core: 2. Of those that a mesh axis runs over, the one named last changes fastest.
Arguments:
- orbitals: bfloat16 [32, 48, 2304], P('orb'), may hold values from -6 to 6
- pair_mask: int32 [2, 32], replicated, may hold values from 0 to 1, as said below
- offsets: int32 [3, 2, 32], replicated, may hold values from -12 to 12
Outputs:
- exchange: bfloat16 [32, 48, 2304], P('orb')
Inputs may be any that keep to these rules, and one draw needn't show every extreme that they name: `pair_mask`: in every matching, the pair that holds orbital 0 and the pair that holds orbital 32 - 1 are live.
All inputs are finite; a program needn't handle non-finite values.
Results may differ from a plain program's by a relative error of at most 0.004.
Values may be sent and summed in bfloat16 or wider, within the bound.
A program may use at most 64 MiB of HBM per device.

v0:
```python
import math

import jax
import jax.numpy as jnp
from jax import lax
from jax.sharding import PartitionSpec as P

screening = 0.5


def from_partner(block, axis, stride):
    count = lax.axis_size(axis)
    route = []
    for low in range(count):
        high = low | 1 << stride
        if high != low and high < count:
            route += [(low, high), (high, low)]
    return lax.ppermute(block, axis, route)


def sine_table(extent):
    modes = jnp.arange(1, extent + 1, dtype=jnp.int32).astype(jnp.float32)
    angles = math.pi * modes[:, None] * modes[None, :] / (extent + 1)
    return math.sqrt(2.0 / (extent + 1)) * jnp.sin(angles)


def inverse_symbol(extent):
    modes = jnp.arange(1, extent + 1, dtype=jnp.int32).astype(jnp.float32)
    eigenvalue = 2.0 - 2.0 * jnp.cos(math.pi * modes / (extent + 1))
    summed_eigen = eigenvalue[:, None, None] + eigenvalue[None, :, None] + eigenvalue[None, None, :]
    return 1.0 / (summed_eigen + screening)


def transform(volume, sines):
    extent = sines.shape[0]
    exact = lax.Precision.HIGHEST
    for turn in range(3):
        flat = jnp.dot(
            sines,
            volume.reshape(extent, extent * extent),
            precision=exact,
            preferred_element_type=jnp.float32,
        )
        volume = jnp.transpose(flat.reshape(extent, extent, extent), (1, 2, 0))
    return volume


def shift_box(volume, offset):
    extent = volume.shape[0]
    places = jnp.arange(extent, dtype=jnp.int32)
    for axis_pos in range(3):
        flat = jnp.roll(volume.reshape(extent, extent * extent), offset[axis_pos], axis=0)
        source = places - offset[axis_pos]
        inside = (source >= 0) & (source < extent)
        flat = jnp.where(inside[:, None], flat, jnp.zeros_like(flat))
        volume = jnp.transpose(flat.reshape(extent, extent, extent), (1, 2, 0))
    return volume


def pair_terms(phi_low, phi_up, offset, sines, symbol):
    visitor = shift_box(phi_up, offset)
    density = phi_low * visitor
    potential = transform(symbol * transform(density, sines), sines)
    lower_term = (potential * visitor).astype(jnp.bfloat16)
    upper_term = shift_box(potential * phi_low, -offset).astype(jnp.bfloat16)
    return (lower_term, upper_term)


def per_device(orbitals, pair_mask, offsets):
    extent = orbitals.shape[1]
    resident = orbitals.reshape(extent, extent, extent)
    sines = sine_table(extent)
    symbol = inverse_symbol(extent)
    devices = lax.axis_size("orb")
    levels = devices.bit_length() - 1
    myself = lax.axis_index("orb")
    matches = pair_mask.shape[0]
    everyone = jnp.arange(devices, dtype=jnp.int32)
    summed = jnp.zeros((extent, extent, extent), jnp.float32)

    def run_pair(operands):
        return pair_terms(*operands)

    def skip_pair(operands):
        nothing = jnp.zeros((extent, extent, extent), jnp.bfloat16)
        return (nothing, nothing)

    for match_index in range(matches):
        bit_pos = match_index * (levels - 1) // (matches - 1)
        stride = 1 << bit_pos
        is_low = myself // stride % 2 == 0
        lower_index = jnp.where(is_low, myself, myself - stride)
        chosen = everyone == lower_index
        live = jnp.sum(jnp.where(chosen, pair_mask[match_index], 0)) > 0
        offset = jnp.sum(jnp.where(chosen[None, :], offsets[:, match_index, :], 0), axis=1)
        partner_orb = from_partner(resident, "orb", bit_pos)
        phi_low = jnp.where(is_low, resident, partner_orb).astype(jnp.float32)
        phi_up = jnp.where(is_low, partner_orb, resident).astype(jnp.float32)
        lower_term, upper_term = lax.cond(
            live, run_pair, skip_pair, (phi_low, phi_up, offset, sines, symbol)
        )
        keeping = jnp.where(is_low, lower_term, upper_term)
        summed = summed + keeping.astype(jnp.float32)
    return (-summed).astype(jnp.bfloat16).reshape(1, extent, extent * extent)


def solution(mesh):
    placed = (P("orb", None, None), P(), P())
    return jax.shard_map(
        per_device, mesh=mesh, in_specs=placed, out_specs=P("orb", None, None), check_vma=False
    )
```

profile of v0, /device:TPU:0, one launch (start us, length us, event | category | flops | bytes accessed | tf_op | source)
XLA Modules:
  0.0 209.0 jit_solution(13131068389292984)
XLA Ops:
  0.0 1.8 reshape.305
  2.3 3.7 %collective-permute-start.1 = (bf16[48,48,48]{2,1,0:T(8,128)(2,1)S(1)}, bf16[48,48,48]{2,1,0:T(8,128)(2,1)}, u32[]{:S(2)}, u32[]{:S(2)}) collective-permute-start(bf16[48,48,48]{2,1,0:T(8,128)(2,1)S(1)} %reshape.305), channel_id=1, source_target_pairs={{0,16},{16,0},{1,17},{17,1},{2,18},{18,2},{3,19},{19,3},{4,20},{20... | collective-permute-start | bytes 663560 | tf_op jit(solution)/shard_map/ppermute | solution.py:18
  10.0 22.6 %collective-permute-done.1 = bf16[48,48,48]{2,1,0:T(8,128)(2,1)} collective-permute-done((bf16[48,48,48]{2,1,0:T(8,128)(2,1)S(1)}, bf16[48,48,48]{2,1,0:T(8,128)(2,1)}, u32[]{:S(2)}, u32[]{:S(2)}) %collective-permute-start.1) | collective-permute-done | bytes 221216 | tf_op jit(solution)/shard_map/ppermute | solution.py:18
  32.6 3.1 %select_convert_fusion.2 = (f32[48,48,48]{2,1,0:T(8,128)}, f32[48,48,48]{2,1,0:T(8,128)S(1)}, f32[48,48,48]{2,1,0:T(8,128)}, f32[48,48,48]{2,1,0:T(8,128)S(1)}) fusion(bf16[48,48,48]{2,1,0:T(8,128)(2,1)} %copy-done.1, bf16[48,48,48]{2,1,0:T(8,128)(2,1)} %copy-done.3, pred[]{:T(512)S(6)} %eq.35, bf16[48,48,48]{2,1,0:T(8,128)(2,1)} %collective-permute-done.1, ...), kind=kLoop, calls=%fused_computation.88 | loop fusion | flops 884736 | bytes 2433026 | tf_op jit(solution)/shard_map/convert_element_type | solution.py:97
  35.8 99.9 %conditional.2 = (bf16[48,48,48]{2,1,0:T(8,128)(2,1)}, bf16[48,48,48]{2,1,0:T(8,128)(2,1)}) conditional(s32[]{:T(128)} %convert_element_type.101, () %tuple.22, (s32[]{:T(128)}, s32[1,32]{1,0:T(1,128)S(1)}, s32[3,2,32]{2,1,0:T(2,128)S(1)}, s32[3,32]{1,0:T(4,128)S(1)}, f32[48,48,48]{2,1,0:T(8,128)S(1)}, /*index=5*/f32[48,48,48]{2,1,0:T(8,128)}, ...), branch_computations={%region_1.2_spmd, %region_2.5_spmd} | conditional | flops 385082752 | bytes 33679100 | solution.py:99
  40.6 1.9 fusion.12
  42.5 1.4 copy.45
  46.9 1.9 fusion.10
  48.8 1.4 copy.46
  52.1 2.0 fusion.8
  55.5 2.4 %mul.24 = f32[48,48,48]{2,1,0:T(8,128)} multiply(f32[48,48,48]{2,1,0:T(8,128)} %get-tuple-element.67, f32[48,48,48]{2,1,0:T(8,128)S(1)} %bitcast.144) | non-fusion elementwise | flops 110592 | bytes 1327104 | tf_op jit(solution)/shard_map/cond/branch_1_fun/mul | solution.py:62
  57.9 2.5 %reshape.263 = f32[48,2304]{1,0:T(8,128)} reshape(f32[48,48,48]{2,1,0:T(8,128)} %mul.24) | data formatting | bytes 884736 | tf_op jit(solution)/shard_map/cond/branch_1_fun/reshape | solution.py:40
  60.4 2.3 %convolution_bitcast_fusion.5 = f32[48,2304]{1,0:T(8,128)} fusion(f32[48,2304]{1,0:T(8,128)} %reshape.263, f32[48,48]{1,0:T(8,128)} %get-tuple-element.78), kind=kOutput, calls=%fused_computation.5 | convolution fusion | flops 63700992 | bytes 893952 | tf_op jit(solution)/shard_map/cond/branch_1_fun/dot_general | solution.py:38
  62.7 2.4 %copy.48 = f32[48,2304]{0,1:T(8,128)} copy(f32[48,2304]{1,0:T(8,128)} %convolution_bitcast_fusion.5) | data formatting | bytes 884736 | tf_op jit(solution)/shard_map/cond/branch_1_fun/reshape | solution.py:44
  65.1 2.5 %reshape.265 = f32[48,2304]{1,0:T(8,128)} reshape(f32[48,48,48]{2,1,0:T(8,128)} %bitcast.156) | data formatting | bytes 884736 | tf_op jit(solution)/shard_map/cond/branch_1_fun/reshape | solution.py:40
  67.6 2.3 %convolution_bitcast_fusion.4 = f32[48,2304]{1,0:T(8,128)} fusion(f32[48,2304]{1,0:T(8,128)} %reshape.265, f32[48,48]{1,0:T(8,128)} %get-tuple-element.78), kind=kOutput, calls=%fused_computation.4 | convolution fusion | flops 63700992 | bytes 893952 | tf_op jit(solution)/shard_map/cond/branch_1_fun/dot_general | solution.py:38
  69.9 2.4 %copy.49 = f32[48,2304]{0,1:T(8,128)} copy(f32[48,2304]{1,0:T(8,128)} %convolution_bitcast_fusion.4) | data formatting | bytes 884736 | tf_op jit(solution)/shard_map/cond/branch_1_fun/reshape | solution.py:44
  72.3 2.5 %reshape.267 = f32[48,2304]{1,0:T(8,128)} reshape(f32[48,48,48]{2,1,0:T(8,128)} %bitcast.157) | data formatting | bytes 884736 | tf_op jit(solution)/shard_map/cond/branch_1_fun/reshape | solution.py:40
  74.8 2.3 %convolution_bitcast_fusion.3 = f32[48,2304]{1,0:T(8,128)} fusion(f32[48,2304]{1,0:T(8,128)} %reshape.267, f32[48,48]{1,0:T(8,128)} %get-tuple-element.78), kind=kOutput, calls=%fused_computation.3 | convolution fusion | flops 63700992 | bytes 893952 | tf_op jit(solution)/shard_map/cond/branch_1_fun/dot_general | solution.py:38
  77.1 2.4 %copy.50 = f32[48,2304]{0,1:T(8,128)} copy(f32[48,2304]{1,0:T(8,128)} %convolution_bitcast_fusion.3) | data formatting | bytes 884736 | tf_op jit(solution)/shard_map/cond/branch_1_fun/reshape | solution.py:44
  79.5 2.4 %mul.25 = f32[48,48,48]{2,1,0:T(8,128)} multiply(f32[48,48,48]{2,1,0:T(8,128)S(1)} %get-tuple-element.66, f32[48,48,48]{2,1,0:T(8,128)} %bitcast.152) | non-fusion elementwise | flops 110592 | bytes 1327104 | tf_op jit(solution)/shard_map/cond/branch_1_fun/mul | solution.py:63
  81.9 2.5 %reshape.269 = f32[48,2304]{1,0:T(8,128)} reshape(f32[48,48,48]{2,1,0:T(8,128)} %mul.25) | data formatting | bytes 884736 | tf_op jit(solution)/shard_map/cond/branch_1_fun/reshape | solution.py:40
  84.4 2.3 %convolution_bitcast_fusion.2 = f32[48,2304]{1,0:T(8,128)} fusion(f32[48,2304]{1,0:T(8,128)} %reshape.269, f32[48,48]{1,0:T(8,128)} %get-tuple-element.78), kind=kOutput, calls=%fused_computation.2 | convolution fusion | flops 63700992 | bytes 893952 | tf_op jit(solution)/shard_map/cond/branch_1_fun/dot_general | solution.py:38
  86.7 2.4 %copy.51 = f32[48,2304]{0,1:T(8,128)} copy(f32[48,2304]{1,0:T(8,128)} %convolution_bitcast_fusion.2) | data formatting | bytes 884736 | tf_op jit(solution)/shard_map/cond/branch_1_fun/reshape | solution.py:44
  89.1 2.5 %reshape.271 = f32[48,2304]{1,0:T(8,128)} reshape(f32[48,48,48]{2,1,0:T(8,128)} %bitcast.158) | data formatting | bytes 884736 | tf_op jit(solution)/shard_map/cond/branch_1_fun/reshape | solution.py:40
  91.6 2.3 %convolution_bitcast_fusion.1 = f32[48,2304]{1,0:T(8,128)} fusion(f32[48,2304]{1,0:T(8,128)} %reshape.271, f32[48,48]{1,0:T(8,128)} %get-tuple-element.78), kind=kOutput, calls=%fused_computation.1 | convolution fusion | flops 63700992 | bytes 893952 | tf_op jit(solution)/shard_map/cond/branch_1_fun/dot_general | solution.py:38
  93.9 2.4 %copy.52 = f32[48,2304]{0,1:T(8,128)} copy(f32[48,2304]{1,0:T(8,128)} %convolution_bitcast_fusion.1) | data formatting | bytes 884736 | tf_op jit(solution)/shard_map/cond/branch_1_fun/reshape | solution.py:44
  96.3 2.5 %reshape.273 = f32[48,2304]{1,0:T(8,128)} reshape(f32[48,48,48]{2,1,0:T(8,128)} %bitcast.159) | data formatting | bytes 884736 | tf_op jit(solution)/shard_map/cond/branch_1_fun/reshape | solution.py:40
  98.8 2.3 %convolution_bitcast_fusion = f32[48,2304]{1,0:T(8,128)} fusion(f32[48,2304]{1,0:T(8,128)} %reshape.273, f32[48,48]{1,0:T(8,128)} %get-tuple-element.78), kind=kOutput, calls=%fused_computation | convolution fusion | flops 63700992 | bytes 893952 | tf_op jit(solution)/shard_map/cond/branch_1_fun/dot_general | solution.py:38
  101.1 2.4 %copy.53 = f32[48,2304]{0,1:T(8,128)} copy(f32[48,2304]{1,0:T(8,128)} %convolution_bitcast_fusion) | data formatting | bytes 884736 | tf_op jit(solution)/shard_map/cond/branch_1_fun/reshape | solution.py:44
  103.5 2.6 %mul.45 = bf16[48,48,48]{2,1,0:T(8,128)(2,1)} multiply(f32[48,48,48]{2,1,0:T(8,128)} %bitcast.148, f32[48,48,48]{2,1,0:T(8,128)} %get-tuple-element.67) | non-fusion elementwise | flops 110592 | bytes 1105920 | tf_op jit(solution)/shard_map/cond/branch_1_fun/mul | solution.py:65
  106.1 2.3 %reshape.275 = bf16[48,2304]{1,0:T(8,128)(2,1)} reshape(bf16[48,48,48]{2,1,0:T(8,128)(2,1)} %mul.45) | data formatting | bytes 442368 | tf_op jit(solution)/shard_map/cond/branch_1_fun/reshape | solution.py:52
  110.2 1.9 fusion.6
  112.1 2.6 %reshape.276 = bf16[48,48,48]{2,1,0:T(8,128)(2,1)} reshape(bf16[48,2304]{1,0:T(8,128)(2,1)} %fusion.6) | data formatting | bytes 442368 | tf_op jit(solution)/shard_map/cond/branch_1_fun/reshape | solution.py:56
  114.6 2.3 %copy.28 = bf16[48,48,48]{2,1,0:T(8,128)(2,1)} copy(bf16[48,48,48]{1,0,2:T(8,128)(2,1)} %bitcast.166) | data formatting | bytes 442368 | tf_op jit(solution)/shard_map/cond/branch_1_fun/transpose | solution.py:56
  117.0 2.3 %reshape.277 = bf16[48,2304]{1,0:T(8,128)(2,1)} reshape(bf16[48,48,48]{2,1,0:T(8,128)(2,1)} %copy.28) | data formatting | bytes 442368 | tf_op jit(solution)/shard_map/cond/branch_1_fun/reshape | solution.py:52
  120.0 1.9 fusion.4
  121.8 2.0 copy.54
  123.8 2.3 %reshape.279 = bf16[48,2304]{1,0:T(8,128)(2,1)} reshape(bf16[48,48,48]{2,1,0:T(8,128)(2,1)} %bitcast.167) | data formatting | bytes 442368 | tf_op jit(solution)/shard_map/cond/branch_1_fun/reshape | solution.py:52
  126.7 1.8 fusion.2
  128.5 2.6 %convert_element_type.72 = bf16[48,48,48]{2,1,0:T(8,128)(2,1)} reshape(bf16[48,2304]{1,0:T(8,128)(2,1)} %fusion.2) | data formatting | bytes 442368 | tf_op jit(solution)/shard_map/cond/branch_1_fun/convert_element_type | solution.py:65
  131.1 2.3 %copy.66 = bf16[48,48,48]{2,1,0:T(8,128)(2,1)} copy(bf16[48,48,48]{1,0,2:T(8,128)(2,1)} %bitcast.168) | data formatting | bytes 442368 | tf_op jit(solution)/shard_map/cond | solution.py:99
  133.4 2.2 %multiply_convert_fusion = bf16[48,48,48]{2,1,0:T(8,128)(2,1)} fusion(f32[48,48,48]{2,1,0:T(8,128)} %bitcast.149, f32[48,48,48]{2,1,0:T(8,128)S(1)} %bitcast.145), kind=kLoop, calls=%fused_computation.6 | loop fusion | flops 221184 | bytes 1105920 | tf_op jit(solution)/shard_map/cond/branch_1_fun/convert_element_type | solution.py:64
  135.6 69.7 %conditional.3 = (bf16[48,48,48]{2,1,0:T(8,128)(2,1)S(1)}, bf16[48,48,48]{2,1,0:T(8,128)(2,1)S(1)}) conditional(s32[]{:T(128)} %convert_element_type.106, () %tuple.24, (s32[]{:T(128)}, s32[1,32]{1,0:T(1,128)S(1)}, s32[3,2,32]{2,1,0:T(2,128)S(1)}, s32[3,32]{1,0:T(4,128)S(1)}, f32[48,48,48]{2,1,0:T(8,128)}, /*index=5*/f32[48,48,48]{2,1,0:T(8,128)S(1)}, ...), branch_computations={%region_5.7_spmd, %region_6.9_spmd} | conditional | flops 385082752 | bytes 33715992 | solution.py:99
  138.9 1.7 reshape.280
  146.1 1.9 fusion.25
  151.3 2.0 fusion.23
  155.9 2.5 %reshape.286 = f32[48,2304]{1,0:T(8,128)} reshape(f32[48,48,48]{2,1,0:T(8,128)} %mul.46) | data formatting | bytes 884736 | tf_op jit(solution)/shard_map/cond/branch_1_fun/reshape | solution.py:40
  158.4 2.3 %convolution_bitcast_fusion.11 = f32[48,2304]{1,0:T(8,128)} fusion(f32[48,2304]{1,0:T(8,128)} %reshape.286, f32[48,48]{1,0:T(8,128)} %get-tuple-element.91), kind=kOutput, calls=%fused_computation.47 | convolution fusion | flops 63700992 | bytes 893952 | tf_op jit(solution)/shard_map/cond/branch_1_fun/dot_general | solution.py:38
  160.7 2.4 %copy.58 = f32[48,2304]{0,1:T(8,128)} copy(f32[48,2304]{1,0:T(8,128)} %convolution_bitcast_fusion.11) | data formatting | bytes 884736 | tf_op jit(solution)/shard_map/cond/branch_1_fun/reshape | solution.py:44
  163.1 2.5 %reshape.288 = f32[48,2304]{1,0:T(8,128)} reshape(f32[48,48,48]{2,1,0:T(8,128)} %bitcast.162) | data formatting | bytes 884736 | tf_op jit(solution)/shard_map/cond/branch_1_fun/reshape | solution.py:40
  165.6 2.3 %convolution_bitcast_fusion.10 = f32[48,2304]{1,0:T(8,128)} fusion(f32[48,2304]{1,0:T(8,128)} %reshape.288, f32[48,48]{1,0:T(8,128)} %get-tuple-element.91), kind=kOutput, calls=%fused_computation.46 | convolution fusion | flops 63700992 | bytes 893952 | tf_op jit(solution)/shard_map/cond/branch_1_fun/dot_general | solution.py:38
  167.9 2.4 %copy.59 = f32[48,2304]{0,1:T(8,128)} copy(f32[48,2304]{1,0:T(8,128)} %convolution_bitcast_fusion.10) | data formatting | bytes 884736 | tf_op jit(solution)/shard_map/cond/branch_1_fun/reshape | solution.py:44
  170.3 2.5 %reshape.290 = f32[48,2304]{1,0:T(8,128)} reshape(f32[48,48,48]{2,1,0:T(8,128)} %bitcast.163) | data formatting | bytes 884736 | tf_op jit(solution)/shard_map/cond/branch_1_fun/reshape | solution.py:40
  172.8 2.3 %convolution_bitcast_fusion.9 = f32[48,2304]{1,0:T(8,128)} fusion(f32[48,2304]{1,0:T(8,128)} %reshape.290, f32[48,48]{1,0:T(8,128)} %get-tuple-element.91), kind=kOutput, calls=%fused_computation.45 | convolution fusion | flops 63700992 | bytes 893952 | tf_op jit(solution)/shard_map/cond/branch_1_fun/dot_general | solution.py:38
  175.1 2.4 %copy.60 = f32[48,2304]{0,1:T(8,128)} copy(f32[48,2304]{1,0:T(8,128)} %convolution_bitcast_fusion.9) | data formatting | bytes 884736 | tf_op jit(solution)/shard_map/cond/branch_1_fun/reshape | solution.py:44
  177.5 2.4 %mul.47 = f32[48,48,48]{2,1,0:T(8,128)} multiply(f32[48,48,48]{2,1,0:T(8,128)S(1)} %get-tuple-element.79, f32[48,48,48]{2,1,0:T(8,128)} %bitcast.153) | non-fusion elementwise | flops 110592 | bytes 1327104 | tf_op jit(solution)/shard_map/cond/branch_1_fun/mul | solution.py:63
  179.9 1.7 reshape.292
  182.9 1.4 copy.61
  185.6 2.3 %convolution_bitcast_fusion.7 = f32[48,2304]{1,0:T(8,128)} fusion(f32[48,2304]{1,0:T(8,128)} %reshape.294, f32[48,48]{1,0:T(8,128)} %get-tuple-element.91), kind=kOutput, calls=%fused_computation.43 | convolution fusion | flops 63700992 | bytes 893952 | tf_op jit(solution)/shard_map/cond/branch_1_fun/dot_general | solution.py:38
  187.9 1.4 copy.62
  190.5 2.3 %convolution_bitcast_fusion.6 = f32[48,2304]{1,0:T(8,128)} fusion(f32[48,2304]{1,0:T(8,128)} %reshape.296, f32[48,48]{1,0:T(8,128)} %get-tuple-element.91), kind=kOutput, calls=%fused_computation.42 | convolution fusion | flops 63700992 | bytes 893952 | tf_op jit(solution)/shard_map/cond/branch_1_fun/dot_general | solution.py:38
  195.2 1.6 reshape.298
  206.2 1.6 negate_convert_fusion
  (70 shorter events, 40.6 us)
Async XLA Ops:
  0.0 6.5 %copy-start.5 = (s32[2,32]{1,0:T(2,128)S(1)}, s32[2,32]{1,0:T(2,128)}, u32[]{:S(2)}) copy-start(s32[2,32]{1,0:T(2,128)} %param.10) | copy-start | bytes 772
  1.8 7.5 %copy-start.1 = (bf16[48,48,48]{2,1,0:T(8,128)(2,1)}, bf16[48,48,48]{2,1,0:T(8,128)(2,1)S(1)}, u32[]{:S(2)}) copy-start(bf16[48,48,48]{2,1,0:T(8,128)(2,1)S(1)} %reshape.305) | copy-start | bytes 663556
  1.8 7.4 %collective-permute-start = (bf16[48,48,48]{2,1,0:T(8,128)(2,1)S(1)}, bf16[48,48,48]{2,1,0:T(8,128)(2,1)S(1)}, u32[]{:S(2)}, u32[]{:S(2)}) collective-permute-start(bf16[48,48,48]{2,1,0:T(8,128)(2,1)S(1)} %reshape.305), channel_id=1, source_target_pairs={{0,1},{1,0},{2,3},{3,2},{4,5},{5,4},{6,7},{7,6},{8,9},{9,8},{10,11... | collective-permute-start | bytes 663560 | tf_op jit(solution)/shard_map/ppermute | solution.py:18
  2.3 30.3 %collective-permute-start.1 = (bf16[48,48,48]{2,1,0:T(8,128)(2,1)S(1)}, bf16[48,48,48]{2,1,0:T(8,128)(2,1)}, u32[]{:S(2)}, u32[]{:S(2)}) collective-permute-start(bf16[48,48,48]{2,1,0:T(8,128)(2,1)S(1)} %reshape.305), channel_id=1, source_target_pairs={{0,16},{16,0},{1,17},{17,1},{2,18},{18,2},{3,19},{19,3},{4,20},{20... | collective-permute-start | bytes 663560 | tf_op jit(solution)/shard_map/ppermute | solution.py:18
  9.2 26.6 %copy-start.4 = (s32[3,2,32]{2,1,0:T(2,128)S(1)}, s32[3,2,32]{2,1,0:T(2,128)}, u32[]{:S(2)}) copy-start(s32[3,2,32]{2,1,0:T(2,128)} %param.11) | copy-start | bytes 2308
  9.2 0.8 copy-start.3
  179.9 1.7 copy-start
  205.3 0.8 copy-start.2
where the time goes:
time: 211 us; the launch traced here: 209 us
  local copies, waits for them, and re-layouts  101 us (48%)
  other arithmetic  45.5 us (22%)
  matrix products  26.5 us (13%)
  waiting for transfers between devices  22.6 us (11%)
  loops' own time  8.37 us (4%)
  starting transfers between devices  4.18 us (2%)
    reshape x12, local copies, waits for them, and re-layouts, transform(): volume.reshape(extent, extent * extent)  26.7 us
    dot_general x12, matrix products, transform(): jnp.dot(sines, volume.reshape(extent, extent * extent), precision=exact,...  26.5 us
    reshape x12, local copies, waits for them, and re-layouts, transform(): volume = jnp.transpose(flat.reshape(extent, extent, extent), (1, 2, 0))  25.8 us
    ppermute x2, waiting for transfers between devices, from_partner(): return lax.ppermute(block, axis, route)  22.6 us
    reshape x12, local copies, waits for them, and re-layouts, shift_box(): volume.reshape(extent, extent * extent)  17.8 us
    select_n x10, other arithmetic, shift_box(): flat = jnp.where(inside[:, None], flat, jnp.zeros_like(flat))  14.9 us
    reshape x10, local copies, waits for them, and re-layouts, shift_box(): volume = jnp.transpose(flat.reshape(extent, extent, extent), (1, 2, 0))  13.9 us
    another operation x2, loops' own time, per_device(): lax.cond(live, run_pair, skip_pair, (phi_low, phi_up, offset, sines, symb...  8.37 us
  transfers between devices with their start and end apart: 2, of which 1 were waited for; matrix products, arithmetic and copies ran while one was open for 1% of the time, Pallas kernels for 0%

commit v1 on v0

v1 whole, which is shorter than its diff:
```python
import functools
import math

import jax
import jax.numpy as jnp
import ml_dtypes
import numpy as np
from jax import lax
from jax.experimental import pallas as pl
from jax.experimental.pallas import tpu as pltpu
from jax.sharding import PartitionSpec as P

screening = 0.5
MESH = pl.DeviceIdType.MESH
NT = (((1,), (1,)), ((), ()))
LANES = 128


def split(values):
    high = values.astype(jnp.bfloat16)
    low = (values - high.astype(jnp.float32)).astype(jnp.bfloat16)
    return high, low


def split_constant(values):
    high = values.astype(ml_dtypes.bfloat16)
    low = (values - high.astype(np.float64)).astype(ml_dtypes.bfloat16)
    return high, low


def tables(extent):
    modes = np.arange(1, extent + 1, dtype=np.float64)
    sines = math.sqrt(2.0 / (extent + 1)) * np.sin(
        math.pi * modes[:, None] * modes[None, :] / (extent + 1)
    )
    eigenvalue = 2.0 - 2.0 * np.cos(math.pi * modes / (extent + 1))
    high, low = split_constant(sines)
    stacked = np.zeros((2 * extent, LANES), ml_dtypes.bfloat16)
    stacked[:extent, :extent] = high
    stacked[extent:, :extent] = low
    width = math.lcm(extent, LANES)
    blocks = np.kron(np.eye(width // extent), sines)
    blocks_high, blocks_low = split_constant(blocks)
    lane = np.arange(extent * extent)
    middle, minor = lane // extent, lane % extent
    eigen_lane = (eigenvalue[middle] + eigenvalue[minor] + screening)[None].astype(np.float32)
    eigen_row = np.broadcast_to(eigenvalue[:, None], (extent, LANES)).astype(np.float32)
    places = np.stack([middle, minor]).astype(np.int32)
    return stacked, blocks_high, blocks_low, eigen_row, eigen_lane, places


def kernel(
    strides,
    pieces,
    offsets_ref,
    mask_ref,
    orbital_ref,
    sines_ref,
    blocks_high_ref,
    blocks_low_ref,
    eigen_row_ref,
    eigen_lane_ref,
    places_ref,
    out_ref,
    own,
    arrived,
    dense,
    slabs,
    symbol,
    load_sem,
    send_sem,
    recv_sem,
):
    extent, cells = own.shape
    width = blocks_high_ref.shape[0]
    myself = lax.axis_index("orb")
    lows = [lax.rem(myself // stride, 2) == 0 for stride in strides]
    partners = [
        jnp.where(low, myself + stride, myself - stride) for low, stride in zip(lows, strides)
    ]

    load = pltpu.make_async_copy(orbital_ref, own, load_sem)
    load.start()
    barrier = pltpu.get_barrier_semaphore()
    for partner in partners:
        pl.semaphore_signal(barrier, inc=1, device_id={"orb": partner}, device_id_type=MESH)
    pl.semaphore_wait(barrier, len(strides))
    rows = extent // pieces
    copies = [[] for _ in strides]
    for match_index in sorted(range(len(strides)), key=lambda at: -strides[at]):
        for piece in range(pieces):
            span = pl.ds(piece * rows, rows)
            copy = pltpu.make_async_remote_copy(
                src_ref=orbital_ref.at[span],
                dst_ref=arrived.at[match_index, span],
                send_sem=send_sem.at[match_index, piece],
                recv_sem=recv_sem.at[match_index, piece],
                device_id={"orb": partners[match_index]},
                device_id_type=MESH,
            )
            copy.start()
            copies[match_index].append(copy)
    load.wait()

    symbol[...] = 1.0 / (eigen_row_ref[:, :1] + eigen_lane_ref[...])
    dense[:, cells:] = jnp.zeros((extent, LANES), jnp.float32)

    def contract_rows(volume):
        high, low = split(volume)
        both = jnp.dot(
            sines_ref[:, :extent], high, preferred_element_type=jnp.float32
        )
        rest = jnp.dot(sines_ref[:extent, :extent], low, preferred_element_type=jnp.float32)
        return both[:extent] + (both[extent:] + rest)

    def contract_lanes(volume):
        chunks = cells // width
        tall = jnp.concatenate(
            [volume[:, at * width : (at + 1) * width] for at in range(chunks)], axis=0
        )
        high, low = split(tall)
        result = jnp.dot(high, blocks_high_ref[...], preferred_element_type=jnp.float32)
        result += jnp.dot(high, blocks_low_ref[...], preferred_element_type=jnp.float32)
        result += jnp.dot(low, blocks_high_ref[...], preferred_element_type=jnp.float32)
        return jnp.concatenate(
            [result[at * extent : (at + 1) * extent] for at in range(chunks)], axis=1
        )

    def rotate(volume):
        dense[:, :cells] = volume
        for at in range(extent):
            slabs[pl.ds(at, extent, stride=extent), :] = dense[:, at * extent : at * extent + LANES]
        high, low = split(slabs[...])
        both = lax.dot_general(sines_ref[...], high, NT, preferred_element_type=jnp.float32)
        rest = lax.dot_general(
            sines_ref[:extent, :], low, NT, preferred_element_type=jnp.float32
        )
        return both[:extent] + (both[extent:] + rest)

    def solve(density):
        spectrum = contract_lanes(rotate(contract_rows(density)))
        return contract_lanes(rotate(rotate(symbol[...] * spectrum)))

    def shift_box(volume, offset):
        row = lax.broadcasted_iota(jnp.int32, (extent, extent), 0)
        column = lax.broadcasted_iota(jnp.int32, (extent, extent), 1)
        pick = jnp.where(row - column == offset[0], 1.0, 0.0).astype(jnp.bfloat16)
        moved = jnp.dot(pick, volume.astype(jnp.bfloat16), preferred_element_type=jnp.float32)
        turn = offset[1] * extent + offset[2]
        moved = pltpu.roll(moved, jnp.where(turn < 0, turn + cells, turn), 1)
        middle = places_ref[0:1, :] - offset[1]
        minor = places_ref[1:2, :] - offset[2]
        inside = (middle >= 0) & (middle < extent) & (minor >= 0) & (minor < extent)
        return jnp.where(inside, moved, 0.0)

    total = None
    for match_index, stride in enumerate(strides):
        is_low = lows[match_index]
        lower = jnp.where(is_low, myself, myself - stride)
        live = mask_ref[match_index, lower]
        offset = [offsets_ref[axis, match_index, lower] for axis in range(3)]
        for copy in copies[match_index]:
            copy.wait_recv()
        mine = own[...].astype(jnp.float32)
        theirs = arrived[match_index].astype(jnp.float32)
        phi_low = jnp.where(is_low, mine, theirs)
        visitor = shift_box(jnp.where(is_low, theirs, mine), offset)
        potential = solve(phi_low * visitor)
        term = (potential * jnp.where(is_low, visitor, phi_low)).astype(jnp.bfloat16)
        term = term.astype(jnp.float32)
        back = [jnp.where(is_low, 0, -value) for value in offset]
        term = jnp.where(live > 0, shift_box(term, back), 0.0)
        total = term if total is None else total + term
    out_ref[...] = (-total).astype(out_ref.dtype)
    for started in copies:
        for copy in started:
            copy.wait_send()


def per_device(orbitals, pair_mask, offsets):
    extent, cells = orbitals.shape[1:]
    levels = lax.axis_size("orb").bit_length() - 1
    matches = pair_mask.shape[0]
    strides = [1 << match_index * (levels - 1) // (matches - 1) for match_index in range(matches)]
    pieces = extent // 16
    vmem = pl.BlockSpec(memory_space=pltpu.VMEM)
    smem = pl.BlockSpec(memory_space=pltpu.SMEM)
    exchange = pl.pallas_call(
        functools.partial(kernel, strides, pieces),
        out_shape=jax.ShapeDtypeStruct((extent, cells), jnp.bfloat16),
        in_specs=[smem, smem, pl.BlockSpec(memory_space=pl.ANY)] + [vmem] * 6,
        out_specs=vmem,
        scratch_shapes=[
            pltpu.VMEM((extent, cells), jnp.bfloat16),
            pltpu.VMEM((matches, extent, cells), jnp.bfloat16),
            pltpu.VMEM((extent, cells + LANES), jnp.float32),
            pltpu.VMEM((cells, LANES), jnp.float32),
            pltpu.VMEM((extent, cells), jnp.float32),
            pltpu.SemaphoreType.DMA,
            pltpu.SemaphoreType.DMA((matches, pieces)),
            pltpu.SemaphoreType.DMA((matches, pieces)),
        ],
        compiler_params=pltpu.CompilerParams(
            collective_id=0, has_side_effects=True, vmem_limit_bytes=40 * 1024 * 1024
        ),
        name="exchange",
    )(offsets, pair_mask, orbitals.reshape(extent, cells), *map(jnp.asarray, tables(extent)))
    return exchange.reshape(1, extent, cells)


def solution(mesh):
    placed = (P("orb", None, None), P(), P())
    return jax.shard_map(
        per_device, mesh=mesh, in_specs=placed, out_specs=P("orb", None, None), check_vma=False
    )
```

time: 211 us -> 29.1 us (0.14)
  local copies, waits for them, and re-layouts: 101 us -> 7.8 us
  other arithmetic: 45.5 us -> 0 us
  matrix products: 26.5 us -> 0 us
  waiting for transfers between devices: 22.6 us -> 0 us
  Pallas kernels: 0 us -> 20.8 us
  loops' own time: 8.37 us -> 0 us
  starting transfers between devices: 4.18 us -> 0 us
    reshape x48 -> x0, local copies, waits for them, and re-layouts: 87.2 us -> none  [the longest x12 26.7 us: transform(): volume.reshape(extent, extent * extent)]
    dot_general x12 -> x0, matrix products: 26.5 us -> none  [transform(): jnp.dot(sines, volume.reshape(extent, extent * extent), precision=exact,...]
    ppermute x2 -> x0, waiting for transfers between devices: 22.6 us -> none  [from_partner(): return lax.ppermute(block, axis, route)]
    pallas_call x0 -> x1, Pallas kernels: none -> 20.8 us  [per_device(): pl.pallas_call(functools.partial(kernel, strides, pieces), out_shape=jax....]
    select_n x10 -> x0, other arithmetic: 14.9 us -> none  [shift_box(): flat = jnp.where(inside[:, None], flat, jnp.zeros_like(flat))]
    mul x8 -> x0, other arithmetic: 12.8 us -> none  [the longest x2 4.87 us: pair_terms(): potential = transform(symbol * transform(density, sines), sines)]
    convert_element_type x7 -> x0, other arithmetic: 9.11 us -> none  [the longest x1 3.13 us: per_device(): phi_low = jnp.where(is_low, resident, partner_orb).astype(jnp.float32)]
    another operation x2 -> x0, loops' own time: 8.37 us -> none  [per_device(): lax.cond(live, run_pair, skip_pair, (phi_low, phi_up, offset, sines, symb...]
  transfers between devices with their start and end apart: 2 -> 0, of which waited for: 1 -> 0; matrix products, arithmetic and copies ran while one was open for 1% -> 0% of each run, Pallas kernels for 0% -> 0%
where the time goes in v1:
time: 29.1 us; the launch traced here: 28.7 us
  Pallas kernels  20.8 us (71%)
  local copies, waits for them, and re-layouts  7.8 us (27%)
    pallas_call x1, Pallas kernels, per_device(): pl.pallas_call(functools.partial(kernel, strides, pieces), out_shape=jax....  20.8 us
    unnamed x19, local copies, waits for them, and re-layouts  7.8 us

profile of v1, /device:TPU:0, one launch (start us, length us, event | category | flops | bytes accessed | tf_op | source)
XLA Modules:
  0.0 28.7 jit_solution(2075360906147767589)
XLA Ops:
  0.0 0.0 copy-start.6
  0.0 0.7 %copy-done.6 = f32[1,2304]{1,0:T(1,128)S(1)} copy-done((f32[1,2304]{1,0:T(1,128)S(1)}, f32[1,2304]{1,0:T(1,128)}, u32[]{:S(2)}) %copy-start.6) | copy-done | bytes 9240
  0.7 0.0 copy-start
  0.7 1.0 %copy-done = bf16[384,384]{1,0:T(8,128)(2,1)S(1)} copy-done((bf16[384,384]{1,0:T(8,128)(2,1)S(1)}, bf16[384,384]{1,0:T(8,128)(2,1)}, u32[]{:S(2)}) %copy-start) | copy-done | bytes 294936
  1.7 0.0 copy-start.1
  1.7 1.0 %copy-done.1 = bf16[384,384]{1,0:T(8,128)(2,1)S(1)} copy-done((bf16[384,384]{1,0:T(8,128)(2,1)S(1)}, bf16[384,384]{1,0:T(8,128)(2,1)}, u32[]{:S(2)}) %copy-start.1) | copy-done | bytes 294936
  2.6 0.0 copy-start.2
  2.6 0.9 %copy-done.2 = bf16[1,48,2304]{2,1,0:T(8,128)(2,1)S(1)} copy-done((bf16[1,48,2304]{2,1,0:T(8,128)(2,1)S(1)}, bf16[1,48,2304]{2,1,0:T(8,128)(2,1)}, u32[]{:S(2)}) %copy-start.2) | copy-done | bytes 221208
  3.6 0.0 copy-start.3
  3.6 0.7 %copy-done.3 = f32[48,128]{1,0:T(8,128)S(1)} copy-done((f32[48,128]{1,0:T(8,128)S(1)}, f32[48,128]{1,0:T(8,128)}, u32[]{:S(2)}) %copy-start.3) | copy-done | bytes 24600
  4.3 0.0 copy-start.4
  4.3 0.7 %copy-done.4 = bf16[96,128]{1,0:T(8,128)(2,1)S(1)} copy-done((bf16[96,128]{1,0:T(8,128)(2,1)S(1)}, bf16[96,128]{1,0:T(8,128)(2,1)}, u32[]{:S(2)}) %copy-start.4) | copy-done | bytes 24600
  5.0 0.0 copy-start.5
  5.0 0.7 %copy-done.5 = s32[2,2304]{1,0:T(2,128)S(1)} copy-done((s32[2,2304]{1,0:T(2,128)S(1)}, s32[2,2304]{1,0:T(2,128)}, u32[]{:S(2)}) %copy-start.5) | copy-done | bytes 18456
  5.8 0.0 copy-start.7
  5.8 0.7 %copy-done.7 = s32[3,2,32]{2,1,0:T(2,128)S(1)} copy-done((s32[3,2,32]{2,1,0:T(2,128)S(1)}, s32[3,2,32]{2,1,0:T(2,128)}, u32[]{:S(2)}) %copy-start.7) | copy-done | bytes 792
  6.4 0.0 copy-start.8
  6.4 0.7 %copy-done.8 = s32[2,32]{1,0:T(2,128)S(1)} copy-done((s32[2,32]{1,0:T(2,128)S(1)}, s32[2,32]{1,0:T(2,128)}, u32[]{:S(2)}) %copy-start.8) | copy-done | bytes 280
  7.1 20.8 %exchange.1 = bf16[48,2304]{1,0:T(8,128)(2,1)S(1)} custom-call(s32[3,2,32]{2,1,0:T(2,128)S(1)} %copy-done.7, s32[2,32]{1,0:T(2,128)S(1)} %copy-done.8, bf16[48,2304]{1,0:T(8,128)(2,1)S(1)} %bitcast.3, bf16[96,128]{1,0:T(8,128)(2,1)S(1)} %copy-done.4, bf16[384,384]{1,0:T(8,128)(2,1)S(1)} %copy-done.1, bf16[384,384]{1,0:T(8,128)(2,1)S(1)} %copy-done, ...), custom_call_target="tpu_custom_call" | custom-call | tf_op jit(solution)/shard_map/exchange/pallas_call | solution.py:188
  28.0 0.7 %copy.11 = bf16[1,48,2304]{2,1,0:T(8,128)(2,1)} copy(bf16[1,48,2304]{2,1,0:T(8,128)(2,1)S(1)} %bitcast.2) | data formatting | bytes 442368
Async XLA Ops:
  0.0 0.7 %copy-start.6 = (f32[1,2304]{1,0:T(1,128)S(1)}, f32[1,2304]{1,0:T(1,128)}, u32[]{:S(2)}) copy-start(f32[1,2304]{1,0:T(1,128)} %constant.16.clone.eigen_lane_ref) | copy-start | bytes 27652
  0.7 1.0 %copy-start = (bf16[384,384]{1,0:T(8,128)(2,1)S(1)}, bf16[384,384]{1,0:T(8,128)(2,1)}, u32[]{:S(2)}) copy-start(bf16[384,384]{1,0:T(8,128)(2,1)} %constant.14.clone.blocks_low_ref) | copy-start | bytes 884740
  1.7 1.0 %copy-start.1 = (bf16[384,384]{1,0:T(8,128)(2,1)S(1)}, bf16[384,384]{1,0:T(8,128)(2,1)}, u32[]{:S(2)}) copy-start(bf16[384,384]{1,0:T(8,128)(2,1)} %constant.13.clone.blocks_high_ref) | copy-start | bytes 884740
  2.6 0.9 %copy-start.2 = (bf16[1,48,2304]{2,1,0:T(8,128)(2,1)S(1)}, bf16[1,48,2304]{2,1,0:T(8,128)(2,1)}, u32[]{:S(2)}) copy-start(bf16[1,48,2304]{2,1,0:T(8,128)(2,1)} %param.9) | copy-start | bytes 663556
  3.6 0.7 %copy-start.3 = (f32[48,128]{1,0:T(8,128)S(1)}, f32[48,128]{1,0:T(8,128)}, u32[]{:S(2)}) copy-start(f32[48,128]{1,0:T(8,128)} %constant.15.clone.eigen_row_ref) | copy-start | bytes 73732
  4.3 0.7 %copy-start.4 = (bf16[96,128]{1,0:T(8,128)(2,1)S(1)}, bf16[96,128]{1,0:T(8,128)(2,1)}, u32[]{:S(2)}) copy-start(bf16[96,128]{1,0:T(8,128)(2,1)} %constant.12.clone.sines_ref) | copy-start | bytes 73732
  5.0 0.7 %copy-start.5 = (s32[2,2304]{1,0:T(2,128)S(1)}, s32[2,2304]{1,0:T(2,128)}, u32[]{:S(2)}) copy-start(s32[2,2304]{1,0:T(2,128)} %constant.17.clone.places_ref) | copy-start | bytes 55300
  5.8 0.7 %copy-start.7 = (s32[3,2,32]{2,1,0:T(2,128)S(1)}, s32[3,2,32]{2,1,0:T(2,128)}, u32[]{:S(2)}) copy-start(s32[3,2,32]{2,1,0:T(2,128)} %offsets_ref.1) | copy-start | bytes 2308
  6.4 0.7 %copy-start.8 = (s32[2,32]{1,0:T(2,128)S(1)}, s32[2,32]{1,0:T(2,128)}, u32[]{:S(2)}) copy-start(s32[2,32]{1,0:T(2,128)} %mask_ref.1) | copy-start | bytes 772

commit v2 on v1

--- a/solution.py
+++ b/solution.py
@@ -52,25 +52,14 @@
 def kernel(
     strides,
     pieces,
-    offsets_ref,
-    mask_ref,
     orbital_ref,
-    sines_ref,
-    blocks_high_ref,
-    blocks_low_ref,
-    eigen_row_ref,
-    eigen_lane_ref,
-    places_ref,
-    out_ref,
-    own,
-    arrived,
-    dense,
-    slabs,
-    symbol,
-    load_sem,
-    send_sem,
-    recv_sem,
+    *refs,
 ):
+    count = (len(refs) - 9) // 2
+    sources, out_ref, held = refs[:count], refs[count], refs[count + 1 : 2 * count + 1]
+    own, arrived, dense, slabs, symbol, load_sem, send_sem, recv_sem = refs[2 * count + 1 :]
+    offsets_ref, mask_ref, sines_ref, blocks_high_ref, blocks_low_ref = held[:5]
+    eigen_row_ref, eigen_lane_ref, places_ref = held[5:]
     extent, cells = own.shape
     width = blocks_high_ref.shape[0]
     myself = lax.axis_index("orb")
@@ -79,11 +68,15 @@
         jnp.where(low, myself + stride, myself - stride) for low, stride in zip(lows, strides)
     ]
 
-    load = pltpu.make_async_copy(orbital_ref, own, load_sem)
-    load.start()
+    loads = [
+        pltpu.make_async_copy(source, target, load_sem.at[at])
+        for at, (source, target) in enumerate(zip((orbital_ref, *sources), (own, *held)))
+    ]
     barrier = pltpu.get_barrier_semaphore()
     for partner in partners:
         pl.semaphore_signal(barrier, inc=1, device_id={"orb": partner}, device_id_type=MESH)
+    for load in loads:
+        load.start()
     pl.semaphore_wait(barrier, len(strides))
     rows = extent // pieces
     copies = [[] for _ in strides]
@@ -100,7 +93,8 @@
             )
             copy.start()
             copies[match_index].append(copy)
-    load.wait()
+    for load in loads:
+        load.wait()
 
     symbol[...] = 1.0 / (eigen_row_ref[:, :1] + eigen_lane_ref[...])
     dense[:, cells:] = jnp.zeros((extent, LANES), jnp.float32)
@@ -183,28 +177,29 @@
     matches = pair_mask.shape[0]
     strides = [1 << match_index * (levels - 1) // (matches - 1) for match_index in range(matches)]
     pieces = extent // 16
-    vmem = pl.BlockSpec(memory_space=pltpu.VMEM)
-    smem = pl.BlockSpec(memory_space=pltpu.SMEM)
+    operands = (offsets, pair_mask, *map(jnp.asarray, tables(extent)))
+    spaces = [pltpu.SMEM] * 2 + [pltpu.VMEM] * (len(operands) - 2)
     exchange = pl.pallas_call(
         functools.partial(kernel, strides, pieces),
         out_shape=jax.ShapeDtypeStruct((extent, cells), jnp.bfloat16),
-        in_specs=[smem, smem, pl.BlockSpec(memory_space=pl.ANY)] + [vmem] * 6,
-        out_specs=vmem,
-        scratch_shapes=[
+        in_specs=[pl.BlockSpec(memory_space=pltpu.HBM)] * (1 + len(operands)),
+        out_specs=pl.BlockSpec(memory_space=pltpu.VMEM),
+        scratch_shapes=[space(one.shape, one.dtype) for space, one in zip(spaces, operands)]
+        + [
             pltpu.VMEM((extent, cells), jnp.bfloat16),
             pltpu.VMEM((matches, extent, cells), jnp.bfloat16),
             pltpu.VMEM((extent, cells + LANES), jnp.float32),
             pltpu.VMEM((cells, LANES), jnp.float32),
             pltpu.VMEM((extent, cells), jnp.float32),
-            pltpu.SemaphoreType.DMA,
+            pltpu.SemaphoreType.DMA((1 + len(operands),)),
             pltpu.SemaphoreType.DMA((matches, pieces)),
             pltpu.SemaphoreType.DMA((matches, pieces)),
         ],
         compiler_params=pltpu.CompilerParams(
-            collective_id=0, has_side_effects=True, vmem_limit_bytes=40 * 1024 * 1024
+            collective_id=0, has_side_effects=True, vmem_limit_bytes=64 * 1024 * 1024
         ),
         name="exchange",
-    )(offsets, pair_mask, orbitals.reshape(extent, cells), *map(jnp.asarray, tables(extent)))
+    )(orbitals.reshape(extent, cells), *operands)
     return exchange.reshape(1, extent, cells)
 
 

time: 29.1 us -> 22.7 us (0.78); the launches traced: 28.7 us -> 22.6 us
  local copies, waits for them, and re-layouts: 7.8 us -> 1.64 us
    unnamed x19 -> x1, local copies, waits for them, and re-layouts: 7.8 us -> 1.64 us
where the time goes in v2:
time: 22.7 us; the launch traced here: 22.6 us
  Pallas kernels  20.9 us (92%)
  local copies, waits for them, and re-layouts  1.64 us (7%)
    pallas_call x1, Pallas kernels, per_device(): pl.pallas_call(functools.partial(kernel, strides, pieces), out_shape=jax....  20.9 us
    unnamed x1, local copies, waits for them, and re-layouts  1.64 us

profile of v2, /device:TPU:0, one launch (start us, length us, event | category | flops | bytes accessed | tf_op | source)
XLA Modules:
  0.0 22.6 jit_solution(14793077458623299391)
XLA Ops:
  0.0 20.9 %exchange.1 = bf16[48,2304]{1,0:T(8,128)(2,1)} custom-call(bf16[48,2304]{1,0:T(8,128)(2,1)} %bitcast.3, s32[3,2,32]{2,1,0:T(2,128)} %refs_0_.1, s32[2,32]{1,0:T(2,128)} %refs_1_.1, bf16[96,128]{1,0:T(8,128)(2,1)} %constant.12.clone.refs_2_, bf16[384,384]{1,0:T(8,128)(2,1)} %constant.13.clone.refs_3_, bf16[384,384]{1,0:T(8,128)(2,1)} %constant.14.clone.refs_4_, ...), custom_call_target="tpu_custom_call" | custom-call | tf_op jit(solution)/shard_map/exchange/pallas_call | solution.py:182
  20.9 1.6 %copy.11 = bf16[1,48,2304]{2,1,0:T(8,128)(2,1)} copy(bf16[1,48,2304]{2,1,0:T(8,128)(2,1)} %bitcast.2) | data formatting | bytes 442368

commit v3 on v2

v3 whole, which is shorter than its diff:
```python
import functools
import math

import jax
import jax.numpy as jnp
import ml_dtypes
import numpy as np
from jax import lax
from jax.experimental import pallas as pl
from jax.experimental.pallas import tpu as pltpu
from jax.sharding import PartitionSpec as P

screening = 0.5
MESH = pl.DeviceIdType.MESH
LANES = 128


def split(values):
    high = values.astype(jnp.bfloat16)
    low = (values - high.astype(jnp.float32)).astype(jnp.bfloat16)
    return high, low


def split_constant(values):
    high = values.astype(ml_dtypes.bfloat16)
    low = (values - high.astype(np.float64)).astype(ml_dtypes.bfloat16)
    return high, low


def tables(extent):
    modes = np.arange(1, extent + 1, dtype=np.float64)
    sines = math.sqrt(2.0 / (extent + 1)) * np.sin(
        math.pi * modes[:, None] * modes[None, :] / (extent + 1)
    )
    eigenvalue = 2.0 - 2.0 * np.cos(math.pi * modes / (extent + 1))
    width = math.lcm(extent, LANES)
    blocks = np.kron(np.eye(width // extent), sines)
    last = np.zeros(LANES)
    last[:extent] = eigenvalue
    eigen_lane = (eigenvalue[:, None] + last[None, :] + screening).reshape(1, extent * LANES)
    eigen_row = np.broadcast_to(eigenvalue[:, None], (extent, LANES))
    lane = np.arange(extent * extent)
    places = np.stack([lane // extent, lane % extent]).astype(np.int32)
    return (
        *split_constant(sines),
        *split_constant(blocks),
        eigen_row.astype(np.float32),
        eigen_lane.astype(np.float32),
        places,
    )


def kernel(
    strides,
    pieces,
    orbital_ref,
    *refs,
):
    count = (len(refs) - 11) // 2
    sources, out_ref, held = refs[:count], refs[count], refs[count + 1 : 2 * count + 1]
    own, arrived, rows_in, rows_out, flat, symbol, moved_own, load_sem, send_sem, recv_sem = refs[
        2 * count + 1 :
    ]
    offsets_ref, mask_ref, sines_high_ref, sines_low_ref, blocks_high_ref, blocks_low_ref = held[:6]
    eigen_row_ref, eigen_lane_ref, places_ref = held[6:]
    extent, cells = own.shape
    width = blocks_high_ref.shape[0]
    myself = lax.axis_index("orb")
    lows = [lax.rem(myself // stride, 2) == 0 for stride in strides]
    partners = [
        jnp.where(low, myself + stride, myself - stride) for low, stride in zip(lows, strides)
    ]

    loads = [
        pltpu.make_async_copy(source, target, load_sem.at[at])
        for at, (source, target) in enumerate(zip((orbital_ref, *sources), (own, *held)))
    ]
    barrier = pltpu.get_barrier_semaphore()
    for partner in partners:
        pl.semaphore_signal(barrier, inc=1, device_id={"orb": partner}, device_id_type=MESH)
    for load in loads:
        load.start()
    pl.semaphore_wait(barrier, len(strides))
    copies = [[] for _ in strides]
    for match_index in sorted(range(len(strides)), key=lambda at: -strides[at]):
        for piece in range(pieces):
            span = pl.ds(piece * width, width)
            copy = pltpu.make_async_remote_copy(
                src_ref=orbital_ref.at[:, span],
                dst_ref=arrived.at[match_index, :, span],
                send_sem=send_sem.at[match_index, piece],
                recv_sem=recv_sem.at[match_index, piece],
                device_id={"orb": partners[match_index]},
                device_id_type=MESH,
            )
            copy.start()
            copies[match_index].append(copy)
    for load in loads:
        load.wait()

    symbol[...] = 1.0 / (eigen_row_ref[:, :1] + eigen_lane_ref[...])
    per_width = width // extent

    def product(left, right):
        return jnp.dot(left, right, preferred_element_type=jnp.float32)

    def side_by_side(high, low):
        return jnp.concatenate([high, low, high], axis=1).astype(jnp.bfloat16)

    row = lax.broadcasted_iota(jnp.int32, (extent, extent), 0)
    column = lax.broadcasted_iota(jnp.int32, (extent, extent), 1)
    wide_row = lax.broadcasted_iota(jnp.int32, (width, width), 0)
    wide_column = lax.broadcasted_iota(jnp.int32, (width, width), 1)
    wide_minor = places_ref[1:2, :width]

    def forward_table(amount):
        pick = jnp.where(row - column == amount, 1.0, 0.0).astype(jnp.bfloat16)
        return side_by_side(product(sines_high_ref[...], pick), product(sines_low_ref[...], pick))

    def inverse_table(amount):
        pick = jnp.where(column - row == amount, 1.0, 0.0).astype(jnp.bfloat16)
        return side_by_side(product(pick, sines_high_ref[...]), product(pick, sines_low_ref[...]))

    def forward_blocks(amount):
        same = (wide_minor >= amount) & (wide_minor < extent + amount)
        pick = jnp.where((wide_column - wide_row == amount) & same, 1.0, 0.0).astype(jnp.bfloat16)
        high, low = product(pick, blocks_high_ref[...]), product(pick, blocks_low_ref[...])
        return high.astype(jnp.bfloat16), low.astype(jnp.bfloat16)

    def inverse_blocks(amount):
        same = (wide_minor >= -amount) & (wide_minor < extent - amount)
        pick = jnp.where((wide_row - wide_column == amount) & same, 1.0, 0.0).astype(jnp.bfloat16)
        high, low = product(blocks_high_ref[...], pick), product(blocks_low_ref[...], pick)
        return high.astype(jnp.bfloat16), low.astype(jnp.bfloat16)

    def contract_rows(table, volume):
        high, low = split(volume)
        return product(table, jnp.concatenate([high, high, low], axis=0))

    def contract_lanes(blocks, volume):
        chunks = volume.shape[1] // width
        tall = [volume[:, at * width : (at + 1) * width] for at in range(chunks)]
        high, low = split(jnp.concatenate(tall, axis=0))
        result = product(high, blocks[0]) + (product(high, blocks[1]) + product(low, blocks[0]))
        parts = [result[at * extent : (at + 1) * extent] for at in range(chunks)]
        return jnp.concatenate(parts, axis=1)

    def shift_box(volume, offset):
        pick = jnp.where(row - column == offset[0], 1.0, 0.0).astype(jnp.bfloat16)
        moved = product(pick, volume)
        turn = offset[1] * extent + offset[2]
        moved = pltpu.roll(moved, jnp.where(turn < 0, turn + cells, turn), 1)
        middle = places_ref[0:1, :] - offset[1]
        minor = places_ref[1:2, :] - offset[2]
        inside = (middle >= 0) & (middle < extent) & (minor >= 0) & (minor < extent)
        return jnp.where(inside, moved, 0.0)

    total = None
    for match_index, stride in enumerate(strides):
        is_low = lows[match_index]
        lower = jnp.where(is_low, myself, myself - stride)
        live = mask_ref[match_index, lower]
        offset = [offsets_ref[axis, match_index, lower] for axis in range(3)]
        ahead = [jnp.where(is_low, value, 0) for value in offset]
        behind = [jnp.where(is_low, 0, value) for value in offset]
        outward = [jnp.where(is_low, -value, value) for value in offset]
        moved_own[...] = shift_box(own[...], outward)
        rows_forward, middle_forward = forward_table(ahead[0]), forward_table(ahead[1])
        rows_inverse, middle_inverse = inverse_table(behind[0]), inverse_table(behind[1])
        lanes_forward, lanes_inverse = forward_blocks(ahead[2]), inverse_blocks(behind[2])

        for piece, copy in enumerate(copies[match_index]):
            copy.wait_recv()
            span = slice(piece * width, (piece + 1) * width)
            density = arrived[match_index, :, span].astype(jnp.float32) * moved_own[:, span]
            part = contract_lanes(lanes_forward, contract_rows(rows_forward, density))
            part = jnp.concatenate([part, part[:, :LANES]], axis=1)
            for at in range(per_width):
                rows_in[pl.ds(piece * per_width + at, extent, stride=extent), :] = part[
                    :, at * extent : at * extent + LANES
                ]
        volume = jnp.concatenate(
            [rows_in[at * extent : (at + 1) * extent, :] for at in range(extent)], axis=1
        )
        volume = symbol[...] * contract_rows(middle_forward, volume)
        volume = contract_rows(middle_inverse, volume)
        for at in range(extent):
            rows_out[at * extent : (at + 1) * extent, :] = volume[:, at * LANES : (at + 1) * LANES]
        for at in range(extent):
            flat[:, at * extent : (at + 1) * extent] = rows_out[
                pl.ds(at, extent, stride=extent), :
            ][:, :extent]
        potential = contract_lanes(lanes_inverse, contract_rows(rows_inverse, flat[...]))
        visitor = shift_box(arrived[match_index], [-value for value in outward])
        term = (potential * visitor).astype(jnp.bfloat16).astype(jnp.float32)
        term = jnp.where(live > 0, term, 0.0)
        total = term if total is None else total + term
    out_ref[...] = (-total).astype(out_ref.dtype)
    for started in copies:
        for copy in started:
            copy.wait_send()


def per_device(orbitals, pair_mask, offsets):
    extent, cells = orbitals.shape[1:]
    levels = lax.axis_size("orb").bit_length() - 1
    matches = pair_mask.shape[0]
    strides = [1 << match_index * (levels - 1) // (matches - 1) for match_index in range(matches)]
    pieces = cells // math.lcm(extent, LANES)
    operands = (offsets, pair_mask, *map(jnp.asarray, tables(extent)))
    spaces = [pltpu.SMEM] * 2 + [pltpu.VMEM] * (len(operands) - 2)
    exchange = pl.pallas_call(
        functools.partial(kernel, strides, pieces),
        out_shape=jax.ShapeDtypeStruct((extent, cells), jnp.bfloat16),
        in_specs=[pl.BlockSpec(memory_space=pltpu.HBM)] * (1 + len(operands)),
        out_specs=pl.BlockSpec(memory_space=pltpu.VMEM),
        scratch_shapes=[space(one.shape, one.dtype) for space, one in zip(spaces, operands)]
        + [
            pltpu.VMEM((extent, cells), jnp.bfloat16),
            pltpu.VMEM((matches, extent, cells), jnp.bfloat16),
            pltpu.VMEM((cells, LANES), jnp.float32),
            pltpu.VMEM((cells, LANES), jnp.float32),
            pltpu.VMEM((extent, cells), jnp.float32),
            pltpu.VMEM((extent, extent * LANES), jnp.float32),
            pltpu.VMEM((extent, cells), jnp.float32),
            pltpu.SemaphoreType.DMA((1 + len(operands),)),
            pltpu.SemaphoreType.DMA((matches, pieces)),
            pltpu.SemaphoreType.DMA((matches, pieces)),
        ],
        compiler_params=pltpu.CompilerParams(
            collective_id=0, has_side_effects=True, vmem_limit_bytes=64 * 1024 * 1024
        ),
        name="exchange",
    )(orbitals.reshape(extent, cells), *operands)
    return exchange.reshape(1, extent, cells)


def solution(mesh):
    placed = (P("orb", None, None), P(), P())
    return jax.shard_map(
        per_device, mesh=mesh, in_specs=placed, out_specs=P("orb", None, None), check_vma=False
    )
```

time: 22.7 us -> 20.3 us (0.89)
  Pallas kernels: 20.9 us -> 18.5 us
    pallas_call x1, Pallas kernels: 20.9 us -> 18.5 us  [per_device(): pl.pallas_call(functools.partial(kernel, strides, pieces), out_shape=jax....]
where the time goes in v3:
time: 20.3 us; the launch traced here: 20.2 us
  Pallas kernels  18.5 us (91%)
  local copies, waits for them, and re-layouts  1.64 us (8%)
    pallas_call x1, Pallas kernels, per_device(): pl.pallas_call(functools.partial(kernel, strides, pieces), out_shape=jax....  18.5 us
    unnamed x1, local copies, waits for them, and re-layouts  1.64 us

profile of v3, /device:TPU:0, one launch (start us, length us, event | category | flops | bytes accessed | tf_op | source)
XLA Modules:
  0.0 20.2 jit_solution(7582602421129925296)
XLA Ops:
  0.0 18.5 %exchange.1 = bf16[48,2304]{1,0:T(8,128)(2,1)} custom-call(bf16[48,2304]{1,0:T(8,128)(2,1)} %bitcast.3, s32[3,2,32]{2,1,0:T(2,128)} %refs_0_.1, s32[2,32]{1,0:T(2,128)} %refs_1_.1, bf16[48,48]{1,0:T(8,128)(2,1)} %constant.14.clone.refs_2_, bf16[48,48]{1,0:T(8,128)(2,1)} %constant.15.clone.refs_3_, bf16[384,384]{1,0:T(8,128)(2,1)} %constant.16.clone.refs_4_, ...), custom_call_target="tpu_custom_call" | custom-call | tf_op jit(solution)/shard_map/exchange/pallas_call | solution.py:212
  18.5 1.6 %copy.12 = bf16[1,48,2304]{2,1,0:T(8,128)(2,1)} copy(bf16[1,48,2304]{2,1,0:T(8,128)(2,1)} %bitcast.2) | data formatting | bytes 442368

commit v4 on v3

--- a/solution.py
+++ b/solution.py
@@ -33,8 +33,8 @@
         math.pi * modes[:, None] * modes[None, :] / (extent + 1)
     )
     eigenvalue = 2.0 - 2.0 * np.cos(math.pi * modes / (extent + 1))
-    width = math.lcm(extent, LANES)
-    blocks = np.kron(np.eye(width // extent), sines)
+    padded = np.zeros((LANES, LANES))
+    padded[:extent, :extent] = sines
     last = np.zeros(LANES)
     last[:extent] = eigenvalue
     eigen_lane = (eigenvalue[:, None] + last[None, :] + screening).reshape(1, extent * LANES)
@@ -43,7 +43,7 @@
     places = np.stack([lane // extent, lane % extent]).astype(np.int32)
     return (
         *split_constant(sines),
-        *split_constant(blocks),
+        *split_constant(padded),
         eigen_row.astype(np.float32),
         eigen_lane.astype(np.float32),
         places,
@@ -61,10 +61,11 @@
     own, arrived, rows_in, rows_out, flat, symbol, moved_own, load_sem, send_sem, recv_sem = refs[
         2 * count + 1 :
     ]
-    offsets_ref, mask_ref, sines_high_ref, sines_low_ref, blocks_high_ref, blocks_low_ref = held[:6]
+    offsets_ref, mask_ref, sines_high_ref, sines_low_ref, padded_high_ref, padded_low_ref = held[:6]
     eigen_row_ref, eigen_lane_ref, places_ref = held[6:]
     extent, cells = own.shape
-    width = blocks_high_ref.shape[0]
+    width = math.lcm(extent, LANES)
+    pieces = cells // width
     myself = lax.axis_index("orb")
     lows = [lax.rem(myself // stride, 2) == 0 for stride in strides]
     partners = [
@@ -109,9 +110,8 @@
 
     row = lax.broadcasted_iota(jnp.int32, (extent, extent), 0)
     column = lax.broadcasted_iota(jnp.int32, (extent, extent), 1)
-    wide_row = lax.broadcasted_iota(jnp.int32, (width, width), 0)
-    wide_column = lax.broadcasted_iota(jnp.int32, (width, width), 1)
-    wide_minor = places_ref[1:2, :width]
+    tile_row = lax.broadcasted_iota(jnp.int32, (LANES, LANES), 0)
+    tile_column = lax.broadcasted_iota(jnp.int32, (LANES, LANES), 1)
 
     def forward_table(amount):
         pick = jnp.where(row - column == amount, 1.0, 0.0).astype(jnp.bfloat16)
@@ -121,29 +121,28 @@
         pick = jnp.where(column - row == amount, 1.0, 0.0).astype(jnp.bfloat16)
         return side_by_side(product(pick, sines_high_ref[...]), product(pick, sines_low_ref[...]))
 
-    def forward_blocks(amount):
-        same = (wide_minor >= amount) & (wide_minor < extent + amount)
-        pick = jnp.where((wide_column - wide_row == amount) & same, 1.0, 0.0).astype(jnp.bfloat16)
-        high, low = product(pick, blocks_high_ref[...]), product(pick, blocks_low_ref[...])
-        return high.astype(jnp.bfloat16), low.astype(jnp.bfloat16)
-
-    def inverse_blocks(amount):
-        same = (wide_minor >= -amount) & (wide_minor < extent - amount)
-        pick = jnp.where((wide_row - wide_column == amount) & same, 1.0, 0.0).astype(jnp.bfloat16)
-        high, low = product(blocks_high_ref[...], pick), product(blocks_low_ref[...], pick)
-        return high.astype(jnp.bfloat16), low.astype(jnp.bfloat16)
+    def lane_table(high, low):
+        high, low = high.astype(jnp.bfloat16), low.astype(jnp.bfloat16)
+        upper = jnp.concatenate([high, low], axis=1)
+        return jnp.concatenate([upper, jnp.concatenate([high, jnp.zeros_like(low)], axis=1)], axis=0)
+
+    def forward_lanes(amount):
+        pick = (tile_column - tile_row == amount) & (tile_row < extent)
+        pick = jnp.where(pick, 1.0, 0.0).astype(jnp.bfloat16)
+        return lane_table(product(pick, padded_high_ref[...]), product(pick, padded_low_ref[...]))
+
+    def inverse_lanes(amount):
+        pick = (tile_row - tile_column == amount) & (tile_column < extent)
+        pick = jnp.where(pick, 1.0, 0.0).astype(jnp.bfloat16)
+        return lane_table(product(padded_high_ref[...], pick), product(padded_low_ref[...], pick))
 
     def contract_rows(table, volume):
         high, low = split(volume)
         return product(table, jnp.concatenate([high, high, low], axis=0))
 
-    def contract_lanes(blocks, volume):
-        chunks = volume.shape[1] // width
-        tall = [volume[:, at * width : (at + 1) * width] for at in range(chunks)]
-        high, low = split(jnp.concatenate(tall, axis=0))
-        result = product(high, blocks[0]) + (product(high, blocks[1]) + product(low, blocks[0]))
-        parts = [result[at * extent : (at + 1) * extent] for at in range(chunks)]
-        return jnp.concatenate(parts, axis=1)
+    def contract_lanes(table, volume):
+        both = product(jnp.concatenate(split(volume), axis=1), table)
+        return both[:, :LANES] + both[:, LANES:]
 
     def shift_box(volume, offset):
         pick = jnp.where(row - column == offset[0], 1.0, 0.0).astype(jnp.bfloat16)
@@ -167,30 +166,34 @@
         moved_own[...] = shift_box(own[...], outward)
         rows_forward, middle_forward = forward_table(ahead[0]), forward_table(ahead[1])
         rows_inverse, middle_inverse = inverse_table(behind[0]), inverse_table(behind[1])
-        lanes_forward, lanes_inverse = forward_blocks(ahead[2]), inverse_blocks(behind[2])
+        lanes_forward, lanes_inverse = forward_lanes(ahead[2]), inverse_lanes(behind[2])
 
         for piece, copy in enumerate(copies[match_index]):
             copy.wait_recv()
             span = slice(piece * width, (piece + 1) * width)
             density = arrived[match_index, :, span].astype(jnp.float32) * moved_own[:, span]
-            part = contract_lanes(lanes_forward, contract_rows(rows_forward, density))
+            part = contract_rows(rows_forward, density)
             part = jnp.concatenate([part, part[:, :LANES]], axis=1)
+            part = [part[:, at * extent : at * extent + LANES] for at in range(per_width)]
+            part = contract_lanes(lanes_forward, jnp.concatenate(part, axis=0))
             for at in range(per_width):
                 rows_in[pl.ds(piece * per_width + at, extent, stride=extent), :] = part[
-                    :, at * extent : at * extent + LANES
+                    at * extent : (at + 1) * extent
                 ]
         volume = jnp.concatenate(
             [rows_in[at * extent : (at + 1) * extent, :] for at in range(extent)], axis=1
         )
         volume = symbol[...] * contract_rows(middle_forward, volume)
         volume = contract_rows(middle_inverse, volume)
-        for at in range(extent):
-            rows_out[at * extent : (at + 1) * extent, :] = volume[:, at * LANES : (at + 1) * LANES]
+        volume = jnp.concatenate(
+            [volume[:, at * LANES : (at + 1) * LANES] for at in range(extent)], axis=0
+        )
+        rows_out[...] = contract_lanes(lanes_inverse, volume)
         for at in range(extent):
             flat[:, at * extent : (at + 1) * extent] = rows_out[
                 pl.ds(at, extent, stride=extent), :
             ][:, :extent]
-        potential = contract_lanes(lanes_inverse, contract_rows(rows_inverse, flat[...]))
+        potential = contract_rows(rows_inverse, flat[...])
         visitor = shift_box(arrived[match_index], [-value for value in outward])
         term = (potential * visitor).astype(jnp.bfloat16).astype(jnp.float32)
         term = jnp.where(live > 0, term, 0.0)
@@ -211,7 +214,7 @@
     spaces = [pltpu.SMEM] * 2 + [pltpu.VMEM] * (len(operands) - 2)
     exchange = pl.pallas_call(
         functools.partial(kernel, strides, pieces),
-        out_shape=jax.ShapeDtypeStruct((extent, cells), jnp.bfloat16),
+        out_shape=pltpu.VMEM((extent, cells), jnp.bfloat16),
         in_specs=[pl.BlockSpec(memory_space=pltpu.HBM)] * (1 + len(operands)),
         out_specs=pl.BlockSpec(memory_space=pltpu.VMEM),
         scratch_shapes=[space(one.shape, one.dtype) for space, one in zip(spaces, operands)]
@@ -228,10 +231,10 @@
             pltpu.SemaphoreType.DMA((matches, pieces)),
         ],
         compiler_params=pltpu.CompilerParams(
-            collective_id=0, has_side_effects=True, vmem_limit_bytes=64 * 1024 * 1024
+            collective_id=0, has_side_effects=True, vmem_limit_bytes=40 * 1024 * 1024
         ),
         name="exchange",
-    )(orbitals.reshape(extent, cells), *operands)
+    )(*(pltpu.with_memory_space_constraint(one, pltpu.HBM) for one in (orbitals.reshape(extent, cells), *operands)))
     return exchange.reshape(1, extent, cells)
 
 

time: 20.3 us -> 18.8 us (0.926)
  local copies, waits for them, and re-layouts: 1.64 us -> 0.69 us
  Pallas kernels: 18.5 us -> 17.9 us
    unnamed x1, local copies, waits for them, and re-layouts: 1.64 us -> 0.69 us
    pallas_call x1, Pallas kernels: 18.5 us -> 17.9 us  [per_device(): pl.pallas_call(functools.partial(kernel, strides, pieces), out_shape=pltp...]
where the time goes in v4:
time: 18.8 us; the launch traced here: 18.6 us
  Pallas kernels  17.9 us (95%)
  local copies, waits for them, and re-layouts  0.69 us (4%)
    pallas_call x1, Pallas kernels, per_device(): pl.pallas_call(functools.partial(kernel, strides, pieces), out_shape=pltp...  17.9 us
    unnamed x1, local copies, waits for them, and re-layouts  0.69 us

profile of v4, /device:TPU:0, one launch (start us, length us, event | category | flops | bytes accessed | tf_op | source)
XLA Modules:
  0.0 18.6 jit_solution(12328069501234800077)
XLA Ops:
  0.0 17.9 %exchange.1 = bf16[48,2304]{1,0:T(8,128)(2,1)S(1)} custom-call(bf16[48,2304]{1,0:T(8,128)(2,1)} %bitcast.3, s32[3,2,32]{2,1,0:T(2,128)} %refs_0_.1, s32[2,32]{1,0:T(2,128)} %refs_1_.1, bf16[48,48]{1,0:T(8,128)(2,1)} %constant.14.clone.refs_2_, bf16[48,48]{1,0:T(8,128)(2,1)} %constant.15.clone.refs_3_, bf16[128,128]{1,0:T(8,128)(2,1)} %constant.16.clone.refs_4_, ...), custom_call_target="tpu_custom_call" | custom-call | tf_op jit(solution)/shard_map/exchange/pallas_call | solution.py:215
  17.9 0.7 %copy.12 = bf16[1,48,2304]{2,1,0:T(8,128)(2,1)} copy(bf16[1,48,2304]{2,1,0:T(8,128)(2,1)S(1)} %bitcast.2) | data formatting | bytes 442368

commit v5 on v4

--- a/solution.py
+++ b/solution.py
@@ -27,17 +27,28 @@
     return high, low
 
 
+def packed(extent):
+    pack = LANES // extent
+    while extent % (8 * pack):
+        pack -= 1
+    return pack
+
+
 def tables(extent):
     modes = np.arange(1, extent + 1, dtype=np.float64)
     sines = math.sqrt(2.0 / (extent + 1)) * np.sin(
         math.pi * modes[:, None] * modes[None, :] / (extent + 1)
     )
     eigenvalue = 2.0 - 2.0 * np.cos(math.pi * modes / (extent + 1))
+    pack = packed(extent)
     padded = np.zeros((LANES, LANES))
-    padded[:extent, :extent] = sines
-    last = np.zeros(LANES)
-    last[:extent] = eigenvalue
-    eigen_lane = (eigenvalue[:, None] + last[None, :] + screening).reshape(1, extent * LANES)
+    padded[: pack * extent, : pack * extent] = np.kron(np.eye(pack), sines)
+    tiles = extent // pack
+    last = np.zeros((tiles, LANES))
+    for at in range(pack):
+        first = eigenvalue[at * tiles : (at + 1) * tiles]
+        last[:, at * extent : (at + 1) * extent] = first[:, None] + eigenvalue[None, :]
+    eigen_lane = (last + screening).reshape(1, tiles * LANES)
     eigen_row = np.broadcast_to(eigenvalue[:, None], (extent, LANES))
     lane = np.arange(extent * extent)
     places = np.stack([lane // extent, lane % extent]).astype(np.int32)
@@ -66,6 +77,8 @@
     extent, cells = own.shape
     width = math.lcm(extent, LANES)
     pieces = cells // width
+    pack = packed(extent)
+    tiles = extent // pack
     myself = lax.axis_index("orb")
     lows = [lax.rem(myself // stride, 2) == 0 for stride in strides]
     partners = [
@@ -112,6 +125,8 @@
     column = lax.broadcasted_iota(jnp.int32, (extent, extent), 1)
     tile_row = lax.broadcasted_iota(jnp.int32, (LANES, LANES), 0)
     tile_column = lax.broadcasted_iota(jnp.int32, (LANES, LANES), 1)
+    tile_minor = places_ref[1:2, :LANES]
+    tile_block = places_ref[0:1, :LANES]
 
     def forward_table(amount):
         pick = jnp.where(row - column == amount, 1.0, 0.0).astype(jnp.bfloat16)
@@ -127,12 +142,14 @@
         return jnp.concatenate([upper, jnp.concatenate([high, jnp.zeros_like(low)], axis=1)], axis=0)
 
     def forward_lanes(amount):
-        pick = (tile_column - tile_row == amount) & (tile_row < extent)
+        inside = (tile_minor >= amount) & (tile_minor < extent + amount)
+        pick = (tile_column - tile_row == amount) & inside
         pick = jnp.where(pick, 1.0, 0.0).astype(jnp.bfloat16)
         return lane_table(product(pick, padded_high_ref[...]), product(pick, padded_low_ref[...]))
 
     def inverse_lanes(amount):
-        pick = (tile_row - tile_column == amount) & (tile_column < extent)
+        inside = (tile_minor >= -amount) & (tile_minor < extent - amount)
+        pick = (tile_row - tile_column == amount) & inside
         pick = jnp.where(pick, 1.0, 0.0).astype(jnp.bfloat16)
         return lane_table(product(padded_high_ref[...], pick), product(padded_low_ref[...], pick))
 
@@ -173,26 +190,35 @@
             span = slice(piece * width, (piece + 1) * width)
             density = arrived[match_index, :, span].astype(jnp.float32) * moved_own[:, span]
             part = contract_rows(rows_forward, density)
-            part = jnp.concatenate([part, part[:, :LANES]], axis=1)
-            part = [part[:, at * extent : at * extent + LANES] for at in range(per_width)]
-            part = contract_lanes(lanes_forward, jnp.concatenate(part, axis=0))
+            part = jnp.concatenate([part[:, -LANES:], part, part[:, :LANES]], axis=1)
+            slabs = []
             for at in range(per_width):
-                rows_in[pl.ds(piece * per_width + at, extent, stride=extent), :] = part[
-                    at * extent : (at + 1) * extent
+                slab = None
+                for lap in range(pack):
+                    start = LANES + (at - lap) * extent
+                    window = part[lap * tiles : (lap + 1) * tiles, start : start + LANES]
+                    slab = window if slab is None else jnp.where(tile_block < lap, slab, window)
+                slabs.append(slab)
+            part = contract_lanes(lanes_forward, jnp.concatenate(slabs, axis=0))
+            for at in range(per_width):
+                rows_in[pl.ds(piece * per_width + at, tiles, stride=extent), :] = part[
+                    at * tiles : (at + 1) * tiles
                 ]
         volume = jnp.concatenate(
-            [rows_in[at * extent : (at + 1) * extent, :] for at in range(extent)], axis=1
+            [rows_in[at * extent : (at + 1) * extent, :] for at in range(tiles)], axis=1
         )
         volume = symbol[...] * contract_rows(middle_forward, volume)
         volume = contract_rows(middle_inverse, volume)
         volume = jnp.concatenate(
-            [volume[:, at * LANES : (at + 1) * LANES] for at in range(extent)], axis=0
+            [volume[:, at * LANES : (at + 1) * LANES] for at in range(tiles)], axis=0
         )
         rows_out[...] = contract_lanes(lanes_inverse, volume)
         for at in range(extent):
-            flat[:, at * extent : (at + 1) * extent] = rows_out[
-                pl.ds(at, extent, stride=extent), :
-            ][:, :extent]
+            slab = rows_out[pl.ds(at, tiles, stride=extent), :]
+            for lap in range(pack):
+                flat[lap * tiles : (lap + 1) * tiles, at * extent : (at + 1) * extent] = slab[
+                    :, lap * extent : (lap + 1) * extent
+                ]
         potential = contract_rows(rows_inverse, flat[...])
         visitor = shift_box(arrived[match_index], [-value for value in outward])
         term = (potential * visitor).astype(jnp.bfloat16).astype(jnp.float32)
@@ -221,10 +247,10 @@
         + [
             pltpu.VMEM((extent, cells), jnp.bfloat16),
             pltpu.VMEM((matches, extent, cells), jnp.bfloat16),
-            pltpu.VMEM((cells, LANES), jnp.float32),
-            pltpu.VMEM((cells, LANES), jnp.float32),
+            pltpu.VMEM((cells // packed(extent), LANES), jnp.float32),
+            pltpu.VMEM((cells // packed(extent), LANES), jnp.float32),
             pltpu.VMEM((extent, cells), jnp.float32),
-            pltpu.VMEM((extent, extent * LANES), jnp.float32),
+            pltpu.VMEM((extent, extent // packed(extent) * LANES), jnp.float32),
             pltpu.VMEM((extent, cells), jnp.float32),
             pltpu.SemaphoreType.DMA((1 + len(operands),)),
             pltpu.SemaphoreType.DMA((matches, pieces)),

time: 18.8 us -> 18.3 us (0.973)
  Pallas kernels: 17.9 us -> 17.4 us
    pallas_call x1, Pallas kernels: 17.9 us -> 17.4 us  [per_device(): pl.pallas_call(functools.partial(kernel, strides, pieces), out_shape=pltp...]
where the time goes in v5:
time: 18.3 us; the launch traced here: 18.1 us
  Pallas kernels  17.4 us (95%)
  local copies, waits for them, and re-layouts  0.69 us (4%)
    pallas_call x1, Pallas kernels, per_device(): pl.pallas_call(functools.partial(kernel, strides, pieces), out_shape=pltp...  17.4 us
    unnamed x1, local copies, waits for them, and re-layouts  0.69 us

profile of v5, /device:TPU:0, one launch (start us, length us, event | category | flops | bytes accessed | tf_op | source)
XLA Modules:
  0.0 18.1 jit_solution(15512013085814136561)
XLA Ops:
  0.0 17.4 %exchange.1 = bf16[48,2304]{1,0:T(8,128)(2,1)S(1)} custom-call(bf16[48,2304]{1,0:T(8,128)(2,1)} %bitcast.3, s32[3,2,32]{2,1,0:T(2,128)} %refs_0_.1, s32[2,32]{1,0:T(2,128)} %refs_1_.1, bf16[48,48]{1,0:T(8,128)(2,1)} %constant.14.clone.refs_2_, bf16[48,48]{1,0:T(8,128)(2,1)} %constant.15.clone.refs_3_, bf16[128,128]{1,0:T(8,128)(2,1)} %constant.16.clone.refs_4_, ...), custom_call_target="tpu_custom_call" | custom-call | tf_op jit(solution)/shard_map/exchange/pallas_call | solution.py:241
  17.4 0.7 %copy.12 = bf16[1,48,2304]{2,1,0:T(8,128)(2,1)} copy(bf16[1,48,2304]{2,1,0:T(8,128)(2,1)S(1)} %bitcast.2) | data formatting | bytes 442368

commit v6 on v5

--- a/solution.py
+++ b/solution.py
@@ -95,20 +95,33 @@
     for load in loads:
         load.start()
     pl.semaphore_wait(barrier, len(strides))
-    copies = [[] for _ in strides]
-    for match_index in sorted(range(len(strides)), key=lambda at: -strides[at]):
-        for piece in range(pieces):
-            span = pl.ds(piece * width, width)
-            copy = pltpu.make_async_remote_copy(
-                src_ref=orbital_ref.at[:, span],
-                dst_ref=arrived.at[match_index, :, span],
+    copies = [
+        [
+            pltpu.make_async_remote_copy(
+                src_ref=orbital_ref.at[:, pl.ds(piece * width, width)],
+                dst_ref=arrived.at[match_index, :, pl.ds(piece * width, width)],
                 send_sem=send_sem.at[match_index, piece],
                 recv_sem=recv_sem.at[match_index, piece],
                 device_id={"orb": partners[match_index]},
                 device_id_type=MESH,
             )
+            for piece in range(pieces)
+        ]
+        for match_index in range(len(strides))
+    ]
+    far = len(strides) - 1
+    yields = lax.rem(myself // max(strides[far] // 2, 1), 4) == 3
+
+    def send(match_index):
+        for copy in copies[match_index]:
             copy.start()
-            copies[match_index].append(copy)
+
+    @pl.when(jnp.logical_not(yields))
+    def _():
+        send(far)
+
+    for match_index in range(far):
+        send(match_index)
     for load in loads:
         load.wait()
 
@@ -184,6 +197,12 @@
         rows_forward, middle_forward = forward_table(ahead[0]), forward_table(ahead[1])
         rows_inverse, middle_inverse = inverse_table(behind[0]), inverse_table(behind[1])
         lanes_forward, lanes_inverse = forward_lanes(ahead[2]), inverse_lanes(behind[2])
+
+        if match_index == min(1, far):
+
+            @pl.when(yields)
+            def _():
+                send(far)
 
         for piece, copy in enumerate(copies[match_index]):
             copy.wait_recv()

time: 18.3 us -> 17.7 us (0.967)
  the two profiles are of different devices: /device:TPU:0 before, /device:TPU:8 now
where the time goes in v6:
time: 17.7 us; the launch traced here: 17.5 us
  Pallas kernels  16.8 us (95%)
  local copies, waits for them, and re-layouts  0.69 us (4%)
    pallas_call x1, Pallas kernels, per_device(): pl.pallas_call(functools.partial(kernel, strides, pieces), out_shape=pltp...  16.8 us
    unnamed x1, local copies, waits for them, and re-layouts  0.69 us

profile of v6, /device:TPU:8, one launch (start us, length us, event | category | flops | bytes accessed | tf_op | source)
XLA Modules:
  0.0 17.5 jit_solution(14181754406984284016)
XLA Ops:
  0.0 16.8 %exchange.1 = bf16[48,2304]{1,0:T(8,128)(2,1)S(1)} custom-call(bf16[48,2304]{1,0:T(8,128)(2,1)} %bitcast.3, s32[3,2,32]{2,1,0:T(2,128)} %refs_0_.1, s32[2,32]{1,0:T(2,128)} %refs_1_.1, bf16[48,48]{1,0:T(8,128)(2,1)} %constant.14.clone.refs_2_, bf16[48,48]{1,0:T(8,128)(2,1)} %constant.15.clone.refs_3_, bf16[128,128]{1,0:T(8,128)(2,1)} %constant.16.clone.refs_4_, ...), custom_call_target="tpu_custom_call" | custom-call | tf_op jit(solution)/shard_map/exchange/pallas_call | solution.py:260
  16.8 0.7 %copy.12 = bf16[1,48,2304]{2,1,0:T(8,128)(2,1)} copy(bf16[1,48,2304]{2,1,0:T(8,128)(2,1)S(1)} %bitcast.2) | data formatting | bytes 442368

commit v7 on v6

--- a/solution.py
+++ b/solution.py
@@ -67,9 +67,9 @@
     orbital_ref,
     *refs,
 ):
-    count = (len(refs) - 11) // 2
+    count = (len(refs) - 12) // 2
     sources, out_ref, held = refs[:count], refs[count], refs[count + 1 : 2 * count + 1]
-    own, arrived, rows_in, rows_out, flat, symbol, moved_own, load_sem, send_sem, recv_sem = refs[
+    own, arrived, rows_in, rows_out, flat, symbol, moved_own, moved_theirs, load_sem, send_sem, recv_sem = refs[
         2 * count + 1 :
     ]
     offsets_ref, mask_ref, sines_high_ref, sines_low_ref, padded_high_ref, padded_low_ref = held[:6]
@@ -110,10 +110,11 @@
         for match_index in range(len(strides))
     ]
     far = len(strides) - 1
+    early = pieces // 3
     yields = lax.rem(myself // max(strides[far] // 2, 1), 4) == 3
 
-    def send(match_index):
-        for copy in copies[match_index]:
+    def send(match_index, part=slice(None)):
+        for copy in copies[match_index][part]:
             copy.start()
 
     @pl.when(jnp.logical_not(yields))
@@ -174,9 +175,11 @@
         both = product(jnp.concatenate(split(volume), axis=1), table)
         return both[:, :LANES] + both[:, LANES:]
 
-    def shift_box(volume, offset):
-        pick = jnp.where(row - column == offset[0], 1.0, 0.0).astype(jnp.bfloat16)
-        moved = product(pick, volume)
+    def shift_rows(volume, amount):
+        pick = jnp.where(row - column == amount, 1.0, 0.0).astype(jnp.bfloat16)
+        return product(pick, volume)
+
+    def shift_lanes(moved, offset):
         turn = offset[1] * extent + offset[2]
         moved = pltpu.roll(moved, jnp.where(turn < 0, turn + cells, turn), 1)
         middle = places_ref[0:1, :] - offset[1]
@@ -193,7 +196,8 @@
         ahead = [jnp.where(is_low, value, 0) for value in offset]
         behind = [jnp.where(is_low, 0, value) for value in offset]
         outward = [jnp.where(is_low, -value, value) for value in offset]
-        moved_own[...] = shift_box(own[...], outward)
+        inward = [-value for value in outward]
+        moved_own[...] = shift_lanes(shift_rows(own[...], outward[0]), outward)
         rows_forward, middle_forward = forward_table(ahead[0]), forward_table(ahead[1])
         rows_inverse, middle_inverse = inverse_table(behind[0]), inverse_table(behind[1])
         lanes_forward, lanes_inverse = forward_lanes(ahead[2]), inverse_lanes(behind[2])
@@ -202,12 +206,14 @@
 
             @pl.when(yields)
             def _():
-                send(far)
+                send(far, slice(early if far else 0, None))
 
         for piece, copy in enumerate(copies[match_index]):
             copy.wait_recv()
             span = slice(piece * width, (piece + 1) * width)
-            density = arrived[match_index, :, span].astype(jnp.float32) * moved_own[:, span]
+            theirs = arrived[match_index, :, span]
+            moved_theirs[:, span] = shift_rows(theirs, inward[0])
+            density = theirs.astype(jnp.float32) * moved_own[:, span]
             part = contract_rows(rows_forward, density)
             part = jnp.concatenate([part[:, -LANES:], part, part[:, :LANES]], axis=1)
             slabs = []
@@ -223,6 +229,12 @@
                 rows_in[pl.ds(piece * per_width + at, tiles, stride=extent), :] = part[
                     at * tiles : (at + 1) * tiles
                 ]
+        if match_index < min(1, far):
+
+            @pl.when(yields)
+            def _():
+                send(far, slice(early))
+
         volume = jnp.concatenate(
             [rows_in[at * extent : (at + 1) * extent, :] for at in range(tiles)], axis=1
         )
@@ -239,7 +251,7 @@
                     :, lap * extent : (lap + 1) * extent
                 ]
         potential = contract_rows(rows_inverse, flat[...])
-        visitor = shift_box(arrived[match_index], [-value for value in outward])
+        visitor = shift_lanes(moved_theirs[...], inward)
         term = (potential * visitor).astype(jnp.bfloat16).astype(jnp.float32)
         term = jnp.where(live > 0, term, 0.0)
         total = term if total is None else total + term
@@ -271,6 +283,7 @@
             pltpu.VMEM((extent, cells), jnp.float32),
             pltpu.VMEM((extent, extent // packed(extent) * LANES), jnp.float32),
             pltpu.VMEM((extent, cells), jnp.float32),
+            pltpu.VMEM((extent, cells), jnp.float32),
             pltpu.SemaphoreType.DMA((1 + len(operands),)),
             pltpu.SemaphoreType.DMA((matches, pieces)),
             pltpu.SemaphoreType.DMA((matches, pieces)),

time: 17.7 us -> 16 us (0.904)
  the two profiles are of different devices: /device:TPU:8 before, /device:TPU:31 now
where the time goes in v7:
time: 16 us; the launch traced here: 15.8 us
  Pallas kernels  15.1 us (94%)
  local copies, waits for them, and re-layouts  0.69 us (4%)
    pallas_call x1, Pallas kernels, per_device(): pl.pallas_call(functools.partial(kernel, strides, pieces), out_shape=pltp...  15.1 us
    unnamed x1, local copies, waits for them, and re-layouts  0.69 us

profile of v7, /device:TPU:31, one launch (start us, length us, event | category | flops | bytes accessed | tf_op | source)
XLA Modules:
  0.0 15.8 jit_solution(16581702994282456237)
XLA Ops:
  0.0 15.1 %exchange.1 = bf16[48,2304]{1,0:T(8,128)(2,1)S(1)} custom-call(bf16[48,2304]{1,0:T(8,128)(2,1)} %bitcast.3, s32[3,2,32]{2,1,0:T(2,128)} %refs_0_.1, s32[2,32]{1,0:T(2,128)} %refs_1_.1, bf16[48,48]{1,0:T(8,128)(2,1)} %constant.14.clone.refs_2_, bf16[48,48]{1,0:T(8,128)(2,1)} %constant.15.clone.refs_3_, bf16[128,128]{1,0:T(8,128)(2,1)} %constant.16.clone.refs_4_, ...), custom_call_target="tpu_custom_call" | custom-call | tf_op jit(solution)/shard_map/exchange/pallas_call | solution.py:272
  15.2 0.7 %copy.12 = bf16[1,48,2304]{2,1,0:T(8,128)(2,1)} copy(bf16[1,48,2304]{2,1,0:T(8,128)(2,1)S(1)} %bitcast.2) | data formatting | bytes 442368

commit v8 on v7

--- a/solution.py
+++ b/solution.py
@@ -167,12 +167,18 @@
         pick = jnp.where(pick, 1.0, 0.0).astype(jnp.bfloat16)
         return lane_table(product(padded_high_ref[...], pick), product(padded_low_ref[...], pick))
 
-    def contract_rows(table, volume):
+    def contract_rows(table, volume, rounded=False):
+        if rounded:
+            high = volume.astype(jnp.bfloat16)
+            return product(table[:, : 2 * extent], jnp.concatenate([high, high], axis=0))
         high, low = split(volume)
         return product(table, jnp.concatenate([high, high, low], axis=0))
 
-    def contract_lanes(table, volume):
-        both = product(jnp.concatenate(split(volume), axis=1), table)
+    def contract_lanes(table, volume, rounded=False):
+        if rounded:
+            both = product(volume.astype(jnp.bfloat16), table[:LANES])
+        else:
+            both = product(jnp.concatenate(split(volume), axis=1), table)
         return both[:, :LANES] + both[:, LANES:]
 
     def shift_rows(volume, amount):
@@ -239,11 +245,11 @@
             [rows_in[at * extent : (at + 1) * extent, :] for at in range(tiles)], axis=1
         )
         volume = symbol[...] * contract_rows(middle_forward, volume)
-        volume = contract_rows(middle_inverse, volume)
+        volume = contract_rows(middle_inverse, volume, rounded=True)
         volume = jnp.concatenate(
             [volume[:, at * LANES : (at + 1) * LANES] for at in range(tiles)], axis=0
         )
-        rows_out[...] = contract_lanes(lanes_inverse, volume)
+        rows_out[...] = contract_lanes(lanes_inverse, volume, rounded=True)
         for at in range(extent):
             slab = rows_out[pl.ds(at, tiles, stride=extent), :]
             for lap in range(pack):

time: 16 us -> 15.9 us (level)
  the two profiles are of different devices: /device:TPU:31 before, /device:TPU:25 now
where the time goes in v8:
time: 15.9 us; the launch traced here: 15.8 us
  Pallas kernels  15.1 us (95%)
  local copies, waits for them, and re-layouts  0.69 us (4%)
    pallas_call x1, Pallas kernels, per_device(): pl.pallas_call(functools.partial(kernel, strides, pieces), out_shape=pltp...  15.1 us
    unnamed x1, local copies, waits for them, and re-layouts  0.69 us

profile of v8, /device:TPU:25, one launch (start us, length us, event | category | flops | bytes accessed | tf_op | source)
XLA Modules:
  0.0 15.8 jit_solution(9863264904650694532)
XLA Ops:
  0.0 15.1 %exchange.1 = bf16[48,2304]{1,0:T(8,128)(2,1)S(1)} custom-call(bf16[48,2304]{1,0:T(8,128)(2,1)} %bitcast.3, s32[3,2,32]{2,1,0:T(2,128)} %refs_0_.1, s32[2,32]{1,0:T(2,128)} %refs_1_.1, bf16[48,48]{1,0:T(8,128)(2,1)} %constant.14.clone.refs_2_, bf16[48,48]{1,0:T(8,128)(2,1)} %constant.15.clone.refs_3_, bf16[128,128]{1,0:T(8,128)(2,1)} %constant.16.clone.refs_4_, ...), custom_call_target="tpu_custom_call" | custom-call | tf_op jit(solution)/shard_map/exchange/pallas_call | solution.py:278
  15.1 0.7 %copy.12 = bf16[1,48,2304]{2,1,0:T(8,128)(2,1)} copy(bf16[1,48,2304]{2,1,0:T(8,128)(2,1)S(1)} %bitcast.2) | data formatting | bytes 442368

commit v9 on v7

--- a/solution.py
+++ b/solution.py
@@ -250,7 +250,13 @@
                 flat[lap * tiles : (lap + 1) * tiles, at * extent : (at + 1) * extent] = slab[
                     :, lap * extent : (lap + 1) * extent
                 ]
-        potential = contract_rows(rows_inverse, flat[...])
+        potential = jnp.concatenate(
+            [
+                contract_rows(rows_inverse, flat[:, at * width : (at + 1) * width])
+                for at in range(pieces)
+            ],
+            axis=1,
+        )
         visitor = shift_lanes(moved_theirs[...], inward)
         term = (potential * visitor).astype(jnp.bfloat16).astype(jnp.float32)
         term = jnp.where(live > 0, term, 0.0)

time: 16 us -> 16 us (level)
  no operation moved by 1% of the time
where the time goes in v9:
time: 16 us; the launch traced here: 15.9 us
  Pallas kernels  15.2 us (95%)
  local copies, waits for them, and re-layouts  0.69 us (4%)
    pallas_call x1, Pallas kernels, per_device(): pl.pallas_call(functools.partial(kernel, strides, pieces), out_shape=pltp...  15.2 us
    unnamed x1, local copies, waits for them, and re-layouts  0.69 us

profile of v9, /device:TPU:31, one launch (start us, length us, event | category | flops | bytes accessed | tf_op | source)
XLA Modules:
  0.0 15.9 jit_solution(6177917883223567436)
XLA Ops:
  0.0 15.2 %exchange.1 = bf16[48,2304]{1,0:T(8,128)(2,1)S(1)} custom-call(bf16[48,2304]{1,0:T(8,128)(2,1)} %bitcast.3, s32[3,2,32]{2,1,0:T(2,128)} %refs_0_.1, s32[2,32]{1,0:T(2,128)} %refs_1_.1, bf16[48,48]{1,0:T(8,128)(2,1)} %constant.14.clone.refs_2_, bf16[48,48]{1,0:T(8,128)(2,1)} %constant.15.clone.refs_3_, bf16[128,128]{1,0:T(8,128)(2,1)} %constant.16.clone.refs_4_, ...), custom_call_target="tpu_custom_call" | custom-call | tf_op jit(solution)/shard_map/exchange/pallas_call | solution.py:278
  15.2 0.7 %copy.12 = bf16[1,48,2304]{2,1,0:T(8,128)(2,1)} copy(bf16[1,48,2304]{2,1,0:T(8,128)(2,1)S(1)} %bitcast.2) | data formatting | bytes 442368
